TPU v7x, 256 devices: a whole 4x4x8 slice. The times are simulated.
256 devices in a mesh: group: 4 (over z_lo, core), tile: 64 (over x, z_hi, y).
Axes of the slice: x: 4, y: 4, z: 8 (z_hi: 4, z_lo: 2; z = z_hi * 2 + z_lo), core: 2. Of those that a mesh axis runs over, the one named last changes fastest.
Arguments:
- object_slices: bfloat16 [4, 2048, 8192], P(None, 'group', 'tile'), may hold values from -4 to 4
- probe: float32 [1024, 256], replicated, may hold values from -6 to 6
- mid_waves: bfloat16 [4, 64, 3, 2, 2, 256, 256], P('group', 'tile'), may hold values from -160 to 160
- amplitudes: bfloat16 [4, 64, 3, 256, 256], P('group', 'tile'), may hold values from 0.19921875 to 4
- row_offsets: int32 [4, 64, 3], P('group', 'tile'), may hold values from 0 to 256
- col_offsets: int32 [4, 64, 3], P('group', 'tile'), may hold values from 0 to 128
Outputs:
- object_new: float32 [4, 2048, 8192], P(None, 'group', 'tile')
- probe_new: float32 [1024, 256], P('tile')
All inputs are finite; a program needn't handle non-finite values.
Results may differ from a plain program's by a relative error of at most 0.0003.
Values may be sent and summed in bfloat16 or wider, within the bound.
A program may use at most 128 MiB of HBM per device.

v0:
```python
import jax
import jax.numpy as jnp
from jax import lax
from jax.sharding import PartitionSpec as P

phase_rate = 0.25
floor_level = 0.5
object_step = 0.5
probe_step = 0.5
epsilon = 1e-06


def with_halo(cells, sides, width):
    for axis, dim in sides:
        count = lax.axis_size(axis)
        ends = count - 1
        head = lax.slice_in_dim(cells, 0, width, axis=dim)
        tail = lax.slice_in_dim(cells, cells.shape[dim] - width, cells.shape[dim], axis=dim)
        cells = jnp.concatenate(
            [
                lax.ppermute(tail, axis, [(i, (i + 1) % count) for i in range(ends)]),
                cells,
                lax.ppermute(head, axis, [((i + 1) % count, i) for i in range(ends)]),
            ],
            axis=dim,
        )
    return cells


def passed_along(block, axis, distance):
    devices = range(lax.axis_size(axis))
    route = [(i - distance, i) for i in devices if i - distance in devices]
    return lax.ppermute(block, axis, route)


def dft_tables(length):
    index = jnp.arange(length, dtype=jnp.int32)
    product = index[:, None] * index[None, :] % length
    angle = product.astype(jnp.float32) * (2.0 * jnp.pi / length)
    norming = 1.0 / jnp.sqrt(jnp.float32(length))
    return (jnp.cos(angle) * norming, jnp.sin(angle) * norming)


def back_tables(length):
    freq = jnp.arange(length, dtype=jnp.int32)
    freq = jnp.where(freq < length // 2, freq, freq - length).astype(jnp.float32)
    phase = (
        2.0
        * jnp.pi
        * phase_rate
        / length
        * (freq[:, None] * freq[:, None] + freq[None, :] * freq[None, :])
    )
    return (jnp.cos(phase), jnp.sin(phase))


def spectral(real_part, imag_part, cos_table, sin_table, direction):
    highest = lax.Precision.HIGHEST
    signed = sin_table * direction
    left_real = jnp.matmul(cos_table, real_part, precision=highest) - jnp.matmul(
        signed, imag_part, precision=highest
    )
    left_imag = jnp.matmul(cos_table, imag_part, precision=highest) + jnp.matmul(
        signed, real_part, precision=highest
    )
    out_real = jnp.matmul(left_real, cos_table, precision=highest) - jnp.matmul(
        left_imag, signed, precision=highest
    )
    out_imag = jnp.matmul(left_imag, cos_table, precision=highest) + jnp.matmul(
        left_real, signed, precision=highest
    )
    return (out_real, out_imag)


def shards(object_slices, probe, mid_waves, amplitudes, row_offsets, col_offsets):
    row_count = object_slices.shape[1]
    strip_width = object_slices.shape[2]
    probe_size = probe.shape[1]
    mode_count = probe.shape[0] // (2 * probe_size)
    padded = with_halo(object_slices, (("tile", 2),), strip_width).astype(jnp.float32)
    probe_parts = probe.reshape(2, mode_count, probe_size, probe_size)
    cos_table, sin_table = dft_tables(probe_size)
    kernel_real, kernel_imag = back_tables(probe_size)
    grad_obj = jnp.zeros(padded.shape, jnp.float32)
    grad_probe = jnp.zeros((2, mode_count, probe_size, probe_size), jnp.float32)
    anchor = jnp.zeros((), jnp.int32)
    for position in range(mid_waves.shape[2]):
        row_at = row_offsets[0, 0, position]
        col_at = col_offsets[0, 0, position]
        patch = lax.dynamic_slice(padded, (anchor, row_at, col_at), (4, probe_size, probe_size))
        first_real, first_imag, second_real, second_imag = (patch[0], patch[1], patch[2], patch[3])
        wave = mid_waves[0, 0, position].astype(jnp.float32)
        mid_real, mid_imag = (wave[0], wave[1])
        amp = amplitudes[0, 0, position].astype(jnp.float32)
        exit_real = mid_real * second_real - mid_imag * second_imag
        exit_imag = mid_real * second_imag + mid_imag * second_real
        far_real, far_imag = spectral(exit_real, exit_imag, cos_table, sin_table, -1.0)
        power = jnp.sum(far_real * far_real + far_imag * far_imag, axis=0)
        factor = 1.0 - amp / jnp.maximum(jnp.sqrt(power), floor_level)
        chi_real, chi_imag = spectral(
            far_real * factor, far_imag * factor, cos_table, sin_table, 1.0
        )
        second_grad_real = jnp.sum(mid_real * chi_real + mid_imag * chi_imag, axis=0)
        second_grad_imag = jnp.sum(mid_real * chi_imag - mid_imag * chi_real, axis=0)
        back_real = second_real * chi_real + second_imag * chi_imag
        back_imag = second_real * chi_imag - second_imag * chi_real
        spec_real, spec_imag = spectral(back_real, back_imag, cos_table, sin_table, -1.0)
        turned_real = spec_real * kernel_real - spec_imag * kernel_imag
        turned_imag = spec_real * kernel_imag + spec_imag * kernel_real
        wave_real, wave_imag = spectral(turned_real, turned_imag, cos_table, sin_table, 1.0)
        first_grad_real = jnp.sum(probe_parts[0] * wave_real + probe_parts[1] * wave_imag, axis=0)
        first_grad_imag = jnp.sum(probe_parts[0] * wave_imag - probe_parts[1] * wave_real, axis=0)
        probe_real = first_real * wave_real + first_imag * wave_imag
        probe_imag = first_real * wave_imag - first_imag * wave_real
        grad_probe = grad_probe + jnp.stack([probe_real, probe_imag])
        update = jnp.stack([first_grad_real, first_grad_imag, second_grad_real, second_grad_imag])
        previous = lax.dynamic_slice(
            grad_obj, (anchor, row_at, col_at), (4, probe_size, probe_size)
        )
        grad_obj = lax.dynamic_update_slice(grad_obj, previous + update, (anchor, row_at, col_at))
    left_rim = grad_obj[:, :, :strip_width]
    right_rim = grad_obj[:, :, 2 * strip_width :]
    own_grad = grad_obj[:, :, strip_width : 2 * strip_width]
    own_grad = own_grad + passed_along(left_rim, "tile", -1)
    own_grad = own_grad + passed_along(right_rim, "tile", 1)
    object_squares = jnp.sum(own_grad * own_grad)
    flat_probe = grad_probe.reshape(2 * mode_count * probe_size, probe_size)
    share = flat_probe.shape[0] // lax.axis_size("tile")
    start_row = lax.axis_index("tile") * share
    probe_total = lax.psum(flat_probe, ("group", "tile"))
    probe_shard = lax.dynamic_slice_in_dim(probe_total, start_row, share, 0)
    object_total = lax.psum(object_squares, ("group", "tile"))
    probe_squares = jnp.sum(probe_total * probe_total)
    object_count = 4 * row_count * strip_width * lax.axis_size("group") * lax.axis_size("tile")
    object_rms = jnp.sqrt(object_total / object_count + epsilon)
    object_new = padded[:, :, strip_width : 2 * strip_width] - object_step * own_grad / object_rms
    probe_count = 2 * mode_count * probe_size * probe_size
    probe_rms = jnp.sqrt(probe_squares / probe_count + epsilon)
    probe_rows = lax.dynamic_slice_in_dim(probe, start_row, share, 0)
    probe_new = probe_rows - probe_step * probe_shard / probe_rms
    return (object_new, probe_new)


def solution(mesh):
    return jax.shard_map(
        shards,
        mesh=mesh,
        in_specs=(
            P(None, "group", "tile"),
            P(),
            P("group", "tile", None, None, None, None, None),
            P("group", "tile", None, None, None),
            P("group", "tile", None),
            P("group", "tile", None),
        ),
        out_specs=(P(None, "group", "tile"), P("tile", None)),
        check_vma=False,
    )
```

profile of v0, /device:TPU:1, one launch (start us, length us, event | category | flops | bytes accessed | tf_op | source)
XLA Modules:
  0.0 642.4 jit_solution(9129326133849237512)
XLA Ops:
  7.2 5.0 collective-permute-start
  32.8 1.7 fusion.122
  34.5 1.7 fusion.126
  36.2 1.7 fusion.182
  37.9 1.7 fusion.186
  39.6 1.7 fusion.152
  41.3 2.0 fusion.156
  43.4 1.7 fusion.6
  45.1 1.7 fusion.7
  51.5 1.7 fusion.22
  53.2 1.7 fusion.23
  54.9 1.7 fusion.184
  59.8 1.7 fusion.14
  61.5 1.7 fusion.15
  66.3 1.8 convolution_subtract_fusion.14
  76.5 1.7 fusion.12
  78.2 2.1 fusion.13
  85.0 2.4 add_reduce_fusion.3
  87.3 1.7 fusion.142
  89.0 1.7 fusion.138
  90.7 1.9 fusion.11
  94.1 1.7 fusion.10
  100.6 1.7 fusion.134
  102.3 1.7 fusion.130
  104.0 1.9 fusion.42
  107.5 1.7 fusion.20
  115.5 2.1 add_reduce_fusion.6
  117.6 1.7 fusion.172
  119.3 1.7 fusion.168
  121.0 1.7 fusion.19
  124.3 1.7 fusion.18
  129.2 1.7 convolution_add_fusion.18
  130.9 1.7 fusion.164
  132.6 1.7 fusion.160
  141.0 1.8 fusion.117
  145.9 2.4 add_reduce_fusion
  148.3 1.7 fusion.112
  150.0 1.7 fusion.108
  151.7 1.7 fusion.3
  153.4 2.0 fusion.110
  155.4 1.7 fusion.2
  161.8 1.7 fusion.104
  163.5 1.7 fusion.100
  165.2 1.7 fusion.9
  166.9 1.7 fusion.132
  168.7 1.7 fusion.8
  175.1 1.7 fusion.17
  176.8 1.7 fusion.16
  178.5 1.8 fusion.158
  183.4 1.7 fusion.1
  186.7 1.7 fusion
  190.0 1.8 convolution_subtract_fusion
  193.4 5.2 add_bitcast_fusion
  199.8 13.5 %dynamic_update_slice.9 = f32[4,512,384]{2,1,0:T(8,128)S(1)} dynamic-update-slice(f32[4,512,384]{2,1,0:T(8,128)S(1)} %broadcast_in_dim.2, f32[4,256,256]{2,1,0:T(8,128)} %pad_maximum_fusion, s32[]{:T(128)} %constant.21.clone.1, s32[]{:T(128)S(6)} %select_n.264, s32[]{:T(128)S(6)} %select_n.265) | dynamic-update-slice | bytes 2097156 | tf_op jit(solution)/shard_map/dynamic_update_slice | solution.py:120
  213.3 2.5 maximum_add_fusion
  215.7 14.7 %dynamic_update_slice.10 = f32[4,512,384]{2,1,0:T(8,128)S(1)} dynamic-update-slice(f32[4,512,384]{2,1,0:T(8,128)S(1)} %dynamic_update_slice.9, f32[4,256,256]{2,1,0:T(8,128)} %maximum_add_fusion, s32[]{:T(128)} %constant.21.clone.1, s32[]{:T(128)S(6)} %select_n.267, s32[]{:T(128)S(6)} %select_n.268) | dynamic-update-slice | bytes 2097156 | tf_op jit(solution)/shard_map/dynamic_update_slice | solution.py:120
  230.4 2.5 maximum_add_fusion.1
  233.0 13.4 %dynamic_update_slice.11 = f32[4,512,384]{2,1,0:T(8,128)S(1)} dynamic-update-slice(f32[4,512,384]{2,1,0:T(8,128)S(1)} %dynamic_update_slice.10, f32[4,256,256]{2,1,0:T(8,128)} %maximum_add_fusion.1, s32[]{:T(128)} %constant.21.clone.1, s32[]{:T(128)S(6)} %select_n.269, s32[]{:T(128)S(6)} %select_n.270) | dynamic-update-slice | bytes 2097156 | tf_op jit(solution)/shard_map/dynamic_update_slice | solution.py:120
  249.4 7.5 %collective-permute-start.3 = (f32[4,512,128]{2,1,0:T(8,128)}, f32[4,512,128]{2,1,0:T(8,128)}, u32[]{:S(2)}, u32[]{:S(2)}) collective-permute-start(f32[4,512,128]{2,1,0:T(8,128)} %get-tuple-element.31), channel_id=1, source_target_pairs={{0,1},{1,2},{2,3},{3,4},{4,5},{5,6},{6,7},{7,8},{8,9},{9,10},{10,1... | collective-permute-start | bytes 3145736 | tf_op jit(solution)/shard_map/ppermute | solution.py:33
  258.1 289.2 %all-reduce.2.cloned.1.call-done = f32[1024,256]{1,0:T(8,128)} async-done(((f32[1024,256]{1,0:T(8,128)}), f32[1024,256]{1,0:T(8,128)}) %all-reduce.2.cloned.1.call-update) | async-done | bytes 1048592 | tf_op jit(solution)/shard_map/psum | solution.py:130
  547.3 2.1 multiply_reduce_fusion
  550.1 2.4 multiply_reduce_fusion.1
  553.9 77.5 %psum.14 = f32[]{:T(128)} all-reduce(f32[]{:T(128)} %multiply_reduce_fusion.1), channel_id=1, replica_groups=mesh['group'=4,'tile'=64] {'group','tile'}, use_global_device_ids=true, to_apply=%region_16.17 | all-reduce | flops 1 | bytes 8 | tf_op jit(solution)/shard_map/psum | solution.py:132
  632.1 3.0 slice_subtract_fusion
  (86 shorter events, 85.7 us)
Async XLA Ops:
  7.2 23.0 %copy-start.7 = (bf16[1,1,3,2,2,256,256]{6,5,4,3,2,1,0:T(8,128)(2,1)S(1)}, bf16[1,1,3,2,2,256,256]{6,5,4,3,2,1,0:T(8,128)(2,1)}, u32[]{:S(2)}) copy-start(bf16[1,1,3,2,2,256,256]{6,5,4,3,2,1,0:T(8,128)(2,1)} %param.8) | copy-start | bytes 4718596
  7.2 540.1 %all-reduce.2.cloned.1.call-start = ((), (), s32[]{:S(2)}) async-start(), calls=%async_computation | async-start | bytes 2097152 | tf_op jit(solution)/shard_map/psum | solution.py:130
  7.2 23.2 %collective-permute-start = (bf16[4,512,128]{2,1,0:T(8,128)(2,1)}, bf16[4,512,128]{2,1,0:T(8,128)(2,1)}, u32[]{:S(2)}, u32[]{:S(2)}) collective-permute-start(bf16[4,512,128]{2,1,0:T(8,128)(2,1)} %param.6), channel_id=1, source_target_pairs={{0,1},{1,2},{2,3},{3,4},{4,5},{5,6},{6,7},{7,8},{8,9},{9,10},{10,1... | collective-permute-start | bytes 1572872 | tf_op jit(solution)/shard_map/ppermute | solution.py:21
  12.2 18.3 %collective-permute-start.1 = (bf16[4,512,128]{2,1,0:T(8,128)(2,1)}, bf16[4,512,128]{2,1,0:T(8,128)(2,1)}, u32[]{:S(2)}, u32[]{:S(2)}) collective-permute-start(bf16[4,512,128]{2,1,0:T(8,128)(2,1)} %param.6), channel_id=1, source_target_pairs={{1,0},{2,1},{3,2},{4,3},{5,4},{6,5},{7,6},{8,7},{9,8},{10,9},{11,1... | collective-permute-start | bytes 1572872 | tf_op jit(solution)/shard_map/ppermute | solution.py:23
  25.3 5.2 copy-start.8
  31.9 13.2 %copy-start = (f32[4,512,384]{2,1,0:T(8,128)}, f32[4,512,384]{2,1,0:T(8,128)S(1)}, u32[]{:S(2)}) copy-start(f32[4,512,384]{2,1,0:T(8,128)S(1)} %maximum_convert_fusion) | copy-start | bytes 9437188
  68.1 4.8 copy-start.9
  246.4 10.5 %copy-start.1 = (f32[1,2,256,256]{3,2,1,0:T(8,128)S(1)}, f32[1,2,256,256]{3,2,1,0:T(8,128)}, u32[]{:S(2)}) copy-start(f32[1,2,256,256]{3,2,1,0:T(8,128)} %get-tuple-element.32) | copy-start | bytes 1572868
  246.4 10.4 %copy-start.2 = (f32[1,2,256,256]{3,2,1,0:T(8,128)S(1)}, f32[1,2,256,256]{3,2,1,0:T(8,128)}, u32[]{:S(2)}) copy-start(f32[1,2,256,256]{3,2,1,0:T(8,128)} %get-tuple-element.33) | copy-start | bytes 1572868
  246.4 10.4 %copy-start.3 = (f32[1,2,256,256]{3,2,1,0:T(8,128)S(1)}, f32[1,2,256,256]{3,2,1,0:T(8,128)}, u32[]{:S(2)}) copy-start(f32[1,2,256,256]{3,2,1,0:T(8,128)} %get-tuple-element.47) | copy-start | bytes 1572868
  246.4 10.4 %copy-start.4 = (f32[1,2,256,256]{3,2,1,0:T(8,128)S(1)}, f32[1,2,256,256]{3,2,1,0:T(8,128)}, u32[]{:S(2)}) copy-start(f32[1,2,256,256]{3,2,1,0:T(8,128)} %get-tuple-element.48) | copy-start | bytes 1572868
  246.4 10.4 %copy-start.5 = (f32[1,2,256,256]{3,2,1,0:T(8,128)S(1)}, f32[1,2,256,256]{3,2,1,0:T(8,128)}, u32[]{:S(2)}) copy-start(f32[1,2,256,256]{3,2,1,0:T(8,128)} %get-tuple-element.49) | copy-start | bytes 1572868
  246.4 10.4 %copy-start.6 = (f32[1,2,256,256]{3,2,1,0:T(8,128)S(1)}, f32[1,2,256,256]{3,2,1,0:T(8,128)}, u32[]{:S(2)}) copy-start(f32[1,2,256,256]{3,2,1,0:T(8,128)} %get-tuple-element.50) | copy-start | bytes 1572868
  248.0 302.1 %collective-permute-start.2 = (f32[4,512,128]{2,1,0:T(8,128)}, f32[4,512,128]{2,1,0:T(8,128)}, u32[]{:S(2)}, u32[]{:S(2)}) collective-permute-start(f32[4,512,128]{2,1,0:T(8,128)} %get-tuple-element.30), channel_id=1, source_target_pairs={{1,0},{2,1},{3,2},{4,3},{5,4},{6,5},{7,6},{8,7},{9,8},{10,9},{11,1... | collective-permute-start | bytes 3145736 | tf_op jit(solution)/shard_map/ppermute | solution.py:33
  249.4 300.7 %collective-permute-start.3 = (f32[4,512,128]{2,1,0:T(8,128)}, f32[4,512,128]{2,1,0:T(8,128)}, u32[]{:S(2)}, u32[]{:S(2)}) collective-permute-start(f32[4,512,128]{2,1,0:T(8,128)} %get-tuple-element.31), channel_id=1, source_target_pairs={{0,1},{1,2},{2,3},{3,4},{4,5},{5,6},{6,7},{7,8},{8,9},{9,10},{10,1... | collective-permute-start | bytes 3145736 | tf_op jit(solution)/shard_map/ppermute | solution.py:33
Sparse Core Ops, SparseCore 0:
  258.2 289.0 all-reduce.1
where the time goes:
time: 653 us; the launch traced here: 642 us
  waiting for transfers between devices  289 us (44%)
  matrix products  165 us (25%)
  blocking collectives  77.5 us (12%)
  local copies, waits for them, and re-layouts  48.4 us (7%)
  between operations  28.3 us (4%)
  other arithmetic  19.1 us (3%)
  starting transfers between devices  15.2 us (2%)
    psum x1, waiting for transfers between devices, shards(): probe_total = lax.psum(flat_probe, ('group', 'tile'))  289 us
    psum x1, blocking collectives, shards(): object_total = lax.psum(object_squares, ('group', 'tile'))  77.5 us
    dynamic_update_slice x3, local copies, waits for them, and re-layouts, shards(): lax.dynamic_update_slice(grad_obj, previous + update, (anchor, row_at, co...  41.6 us
    dot_general x12, matrix products, spectral(): jnp.matmul(left_imag, signed, precision=highest)  22.9 us
    dot_general x12, matrix products, spectral(): jnp.matmul(left_real, signed, precision=highest)  21.2 us
    dot_general x12, matrix products, spectral(): jnp.matmul(signed, imag_part, precision=highest)  20.8 us
    dot_general x12, matrix products, spectral(): jnp.matmul(cos_table, real_part, precision=highest)  20.7 us
    dot_general x12, matrix products, spectral(): jnp.matmul(signed, real_part, precision=highest)  20.2 us
  transfers between devices with their start and end apart: 5, of which 1 were waited for; matrix products, arithmetic and copies ran while one was open for 1% of the time, Pallas kernels for 0%

commit v1 on v0

v1 whole, which is shorter than its diff:
```python
import numpy as np
import ml_dtypes
import jax
import jax.numpy as jnp
from jax import lax
from jax.sharding import PartitionSpec as P
from jax.experimental import pallas as pl
from jax.experimental.pallas import tpu as pltpu

phase_rate = 0.25
floor_level = 0.5
object_step = 0.5
probe_step = 0.5
epsilon = 1e-06
f32 = jnp.float32
bf16 = jnp.bfloat16
PX = 256
HALF = 128
TALL = PX + 8


def right_form(m):
    return np.block([[m.real, m.imag], [-m.imag, m.real]])


def left_form(m):
    return np.block([[m.real, -m.imag], [m.imag, m.real]])


def transform_tables():
    n = np.arange(HALF)[:, None]
    k = np.arange(HALF)[None, :]
    root = -2j * np.pi / PX
    even = np.exp(root * ((2 * n * k) % PX)) / np.sqrt(PX)
    odd = np.exp(root * ((n * (2 * k + 1)) % PX)) / np.sqrt(PX)
    freq = np.arange(PX)
    freq = np.where(freq < HALF, freq, freq - PX)
    phase = np.exp(2j * np.pi * phase_rate * freq * freq / PX)
    ring = np.fft.ifft(phase)
    i, j = np.meshgrid(np.arange(HALF), np.arange(HALF), indexing="ij")
    near, far = ring[(i - j) % PX], ring[(i - j + HALF) % PX]
    plus, minus = (near + far) / 2, (near - far) / 2
    forms = [
        right_form(even), right_form(odd),
        left_form(even.T), left_form(odd.T),
        left_form(even.conj()), left_form(odd.conj()),
        right_form(even.conj().T), right_form(odd.conj().T),
        right_form(plus.T), right_form(minus.T),
        left_form(plus), left_form(minus),
    ]
    whole = np.stack(forms)
    high = whole.astype(ml_dtypes.bfloat16)
    low = (whole - high.astype(np.float64)).astype(ml_dtypes.bfloat16)
    return np.stack([high, low], axis=1)


def split(x):
    high = x.astype(bf16)
    return high, (x - high.astype(f32)).astype(bf16)


def by_right(x, tables, index):
    high, low = split(x)
    t = tables[index, 0]
    return jnp.dot(
        jnp.concatenate([high, low, high], axis=1),
        jnp.concatenate([t, t, tables[index, 1]], axis=0),
        preferred_element_type=f32,
    )


def by_left(x, tables, index):
    high, low = split(x)
    t = tables[index, 0]
    return jnp.dot(
        jnp.concatenate([t, t, tables[index, 1]], axis=1),
        jnp.concatenate([high, low, high], axis=0),
        preferred_element_type=f32,
    )


def lanes(a, b):
    return jnp.concatenate([a, b], axis=1)


def rows(a, b):
    return jnp.concatenate([a, b], axis=0)


def halves(re, im):
    return lanes(re[:, :HALF], im[:, :HALF]), lanes(re[:, HALF:], im[:, HALF:])


def compute_kernel(row_ref, col_ref, mid_obj, left_obj, right_obj, probe, waves, amps, tables,
                   own, left_rim, right_rim, grad_probe,
                   obj, grad, patch, far, upd):
    obj[:, :512, :HALF] = left_obj[...].astype(f32)
    obj[:, :512, HALF : 2 * HALF] = mid_obj[...].astype(f32)
    obj[:, :512, 2 * HALF :] = right_obj[...].astype(f32)
    obj[:, 512:, :] = jnp.zeros((4, 8, 3 * HALF), f32)
    grad[...] = jnp.zeros_like(grad)
    grad_probe[...] = jnp.zeros_like(grad_probe)
    at_row = lax.broadcasted_iota(jnp.int32, (PX, PX), 0)
    at_col = lax.broadcasted_iota(jnp.int32, (PX, PX), 1)
    sort_row = (at_col == jnp.where(at_row < HALF, 2 * at_row, 2 * at_row - PX + 1)).astype(f32).astype(bf16)
    sort_col = (at_row == jnp.where(at_col < HALF, 2 * at_col, 2 * at_col - PX + 1)).astype(f32).astype(bf16)

    def visit(p, carry):
        row_at = row_ref[p]
        col_at = col_ref[p]
        row_base = pl.multiple_of(row_at // 8 * 8, 8)
        row_rest = row_at - row_base
        pick = (
            lax.broadcasted_iota(jnp.int32, (3 * HALF, PX), 0)
            == lax.broadcasted_iota(jnp.int32, (3 * HALF, PX), 1) + col_at
        ).astype(f32).astype(bf16)
        place = (
            lax.broadcasted_iota(jnp.int32, (PX, 3 * HALF), 1)
            == lax.broadcasted_iota(jnp.int32, (PX, 3 * HALF), 0) + col_at
        ).astype(f32).astype(bf16)
        for c in range(4):
            raw = obj[c, pl.ds(row_base, TALL), :].astype(bf16)
            wide = jnp.dot(raw, pick, preferred_element_type=f32)
            patch[c] = pltpu.roll(wide, TALL - row_rest, 0)[:PX]
        for m in range(2):
            sr, si = patch[2], patch[3]
            wr, wi = waves[p, 0, m].astype(f32), waves[p, 1, m].astype(f32)
            p0, p1 = halves(wr * sr - wi * si, wr * si + wi * sr)
            ye = by_right(p0 + p1, tables, 0)
            yo = by_right(p0 - p1, tables, 1)
            re = lanes(ye[:, :HALF], yo[:, :HALF])
            im = lanes(ye[:, HALF:], yo[:, HALF:])
            far[m, 0] = by_left(rows(re[:HALF] + re[HALF:], im[:HALF] + im[HALF:]), tables, 2)
            far[m, 1] = by_left(rows(re[:HALF] - re[HALF:], im[:HALF] - im[HALF:]), tables, 3)
        amp = jnp.dot(sort_row, amps[p], preferred_element_type=f32).astype(bf16)
        amp = jnp.dot(amp, sort_col, preferred_element_type=f32)
        for e in range(2):
            power = 0.0
            for m in range(2):
                z = far[m, e]
                power = power + z[:HALF] * z[:HALF] + z[HALF:] * z[HALF:]
            factor = 1.0 - amp[e * HALF : (e + 1) * HALF] * jnp.minimum(lax.rsqrt(power), 1.0 / floor_level)
            factor = rows(factor, factor)
            for m in range(2):
                far[m, e] = far[m, e] * factor
        for m in range(2):
            u = by_left(far[m, 0], tables, 4)
            v = by_left(far[m, 1], tables, 5)
            s, d = u + v, u - v
            re = rows(s[:HALF], d[:HALF])
            im = rows(s[HALF:], d[HALF:])
            ie, io = halves(re, im)
            u = by_right(ie, tables, 6)
            v = by_right(io, tables, 7)
            s, d = u + v, u - v
            cr = lanes(s[:, :HALF], d[:, :HALF])
            ci = lanes(s[:, HALF:], d[:, HALF:])
            sr, si = patch[2], patch[3]
            wr, wi = waves[p, 0, m].astype(f32), waves[p, 1, m].astype(f32)
            gr, gi = wr * cr + wi * ci, wr * ci - wi * cr
            if m == 0:
                upd[2], upd[3] = gr, gi
            else:
                upd[2], upd[3] = upd[2] + gr, upd[3] + gi
            p0, p1 = halves(sr * cr + si * ci, sr * ci - si * cr)
            u = by_right(p0 + p1, tables, 8)
            v = by_right(p0 - p1, tables, 9)
            s, d = u + v, u - v
            re = lanes(s[:, :HALF], d[:, :HALF])
            im = lanes(s[:, HALF:], d[:, HALF:])
            u = by_left(rows(re[:HALF] + re[HALF:], im[:HALF] + im[HALF:]), tables, 10)
            v = by_left(rows(re[:HALF] - re[HALF:], im[:HALF] - im[HALF:]), tables, 11)
            s, d = u + v, u - v
            br = rows(s[:HALF], d[:HALF])
            bi = rows(s[HALF:], d[HALF:])
            pr, pi = probe[0, m], probe[1, m]
            gr, gi = pr * br + pi * bi, pr * bi - pi * br
            if m == 0:
                upd[0], upd[1] = gr, gi
            else:
                upd[0], upd[1] = upd[0] + gr, upd[1] + gi
            ar, ai = patch[0], patch[1]
            grad_probe[0, m] = grad_probe[0, m] + (ar * br + ai * bi)
            grad_probe[1, m] = grad_probe[1, m] + (ar * bi - ai * br)
        for c in range(4):
            high, low = split(upd[c])
            moved = jnp.dot(lanes(high, low), rows(place, place), preferred_element_type=f32)
            moved = rows(moved, jnp.zeros((TALL - PX, 3 * HALF), f32))
            moved = pltpu.roll(moved, row_rest, 0)
            grad[c, pl.ds(row_base, TALL), :] = grad[c, pl.ds(row_base, TALL), :] + moved
        return carry

    lax.fori_loop(0, row_ref.shape[0], visit, 0)
    left_rim[...] = grad[:, :512, :HALF]
    own[...] = grad[:, :512, HALF : 2 * HALF]
    right_rim[...] = grad[:, :512, 2 * HALF :]


def compute(mid_obj, left_obj, right_obj, probe, waves, amps, row_at, col_at):
    tables = jnp.asarray(transform_tables())
    strip = jax.ShapeDtypeStruct(mid_obj.shape, f32)
    vmem = pl.BlockSpec(memory_space=pltpu.VMEM)
    smem = pl.BlockSpec(memory_space=pltpu.SMEM)
    return pl.pallas_call(
        compute_kernel,
        out_shape=[strip, strip, strip, jax.ShapeDtypeStruct((2, 2, PX, PX), f32)],
        in_specs=[smem, smem] + [vmem] * 7,
        out_specs=[vmem] * 4,
        scratch_shapes=[
            pltpu.VMEM((4, 520, 3 * HALF), f32),
            pltpu.VMEM((4, 520, 3 * HALF), f32),
            pltpu.VMEM((4, PX, PX), f32),
            pltpu.VMEM((2, 2, PX, PX), f32),
            pltpu.VMEM((4, PX, PX), f32),
        ],
        compiler_params=pltpu.CompilerParams(vmem_limit_bytes=60 * 1024 * 1024),
        name="gradient",
    )(row_at, col_at, mid_obj, left_obj, right_obj, probe, waves, amps, tables)


def exchange_kernel(own, left_rim, right_rim, probe_sum, total_out, shard_out, squares_out,
                    from_right, from_left, pieces, r1, s1, r2, s2, r3, s3, r4, fin, q1, q2,
                    rim_sems, pair_sems, sems3, sems4, sems5, sems6, sems7):
    g = lax.axis_index("group")
    t = lax.axis_index("tile")
    layer, core = g // 2, g % 2
    x, zy = t // 16, t % 16
    spot = x * 4 + g
    right = (g, (t + 1) % 64)
    left = (g, (t + 63) % 64)
    other_core = (layer * 2 + 1 - core, t)
    other_layer = ((1 - layer) * 2 + core, t)

    def along_x(j):
        return (g, (x + j) % 4 * 16 + zy)

    def along_zy(j):
        return (g, x * 16 + (zy + j) % 16)

    def along_group(j):
        return ((g + j) % 4, t)

    def along_spot(j):
        to = (spot + j) % 16
        return (to % 4, to // 4 * 16 + zy)

    barrier = pltpu.get_barrier_semaphore()
    partners = [right, left] + [along_zy(j) for j in range(1, 16)] + [along_spot(j) for j in range(1, 16)]
    for partner in partners:
        pl.semaphore_signal(barrier, inc=1, device_id=partner, device_id_type=pl.DeviceIdType.MESH)
    pl.semaphore_wait(barrier, len(partners))

    def send(src, dst, sems, device):
        copy = pltpu.make_async_remote_copy(
            src_ref=src, dst_ref=dst, send_sem=sems.at[0], recv_sem=sems.at[1],
            device_id=device, device_id_type=pl.DeviceIdType.MESH,
        )
        copy.start()
        return copy

    rim_copies = [
        send(left_rim, from_right, rim_sems.at[0], left),
        send(right_rim, from_left, rim_sems.at[1], right),
    ]
    for h in range(2):
        pieces[h] = probe_sum[:, h * HALF : (h + 1) * HALF].reshape(64, 2, 8, HALF)
    copy = send(pieces.at[1 - core], r1, pair_sems.at[0], other_core)
    copy.wait()
    for l in range(2):
        s1[l] = pieces[core, :, l] + r1[:, l]
    copy = send(s1.at[1 - layer], r2, pair_sems.at[1], other_layer)
    copy.wait()
    s2[...] = s1[layer] + r2[...]
    copies = []
    for j in range(1, 4):
        away = pl.multiple_of((x + j) % 4 * 16, 16)
        copies.append(send(s2.at[pl.ds(away, 16)], r3.at[j - 1], sems3.at[j - 1], along_x(j)))
    for copy in copies:
        copy.wait()
    s3[...] = s2[pl.ds(pl.multiple_of(x * 16, 16), 16)] + r3[0] + r3[1] + r3[2]
    copies = []
    for j in range(1, 16):
        copies.append(send(s3.at[(zy + j) % 16], r4.at[j - 1], sems4.at[j - 1], along_zy(j)))
    for copy in copies:
        copy.wait()
    piece = s3[zy]
    for j in range(15):
        piece = piece + r4[j]
    fin[0] = piece
    gathers = [send(fin.at[0], fin.at[j], sems5.at[j - 1], along_group(j)) for j in range(1, 4)]
    for copy in rim_copies:
        copy.wait()
    with_right = jnp.where(t < 63, 1.0, 0.0)
    with_left = jnp.where(t > 0, 1.0, 0.0)
    acc = jnp.zeros((8, HALF), f32)
    for c in range(4):
        total = own[c] + from_right[c] * with_right + from_left[c] * with_left
        total_out[c] = total
        acc = acc + jnp.sum((total * total).reshape(64, 8, HALF), axis=0)
    object_row = jnp.sum(acc, axis=0, keepdims=True)
    probe_row = jnp.sum(piece * piece, axis=0, keepdims=True)
    top = lax.broadcasted_iota(jnp.int32, (8, HALF), 0) < 4
    q1[0] = jnp.where(top, object_row, probe_row)
    copies = [send(q1.at[0], q1.at[j], sems6.at[j - 1], along_zy(j)) for j in range(1, 16)]
    for copy in copies:
        copy.wait()
    both = q1[zy]
    for s in range(1, 16):
        both = both + q1[(zy + 16 - s) % 16]
    q2[0] = both
    copies = [send(q2.at[0], q2.at[j], sems7.at[j - 1], along_spot(j)) for j in range(1, 16)]
    for copy in copies:
        copy.wait()
    both = q2[spot]
    for s in range(1, 16):
        both = both + q2[(spot + 16 - s) % 16]
    squares_out[...] = both
    for copy in gathers:
        copy.wait()
    for s in range(4):
        shard_out[s // 2 * 8 : s // 2 * 8 + 8, s % 2 * HALF : s % 2 * HALF + HALF] = fin[(g + 4 - s) % 4]


def exchange(own, left_rim, right_rim, probe_sum):
    strip = own.shape
    tile = (8, HALF)
    vmem = pl.BlockSpec(memory_space=pltpu.VMEM)
    sem = pltpu.SemaphoreType.DMA
    return pl.pallas_call(
        exchange_kernel,
        out_shape=[
            jax.ShapeDtypeStruct(strip, f32),
            jax.ShapeDtypeStruct((16, PX), f32),
            jax.ShapeDtypeStruct(tile, f32),
        ],
        in_specs=[vmem] * 4,
        out_specs=[vmem] * 3,
        scratch_shapes=[
            pltpu.VMEM(strip, f32),
            pltpu.VMEM(strip, f32),
            pltpu.VMEM((2, 64, 2, *tile), f32),
            pltpu.VMEM((64, 2, *tile), f32),
            pltpu.VMEM((2, 64, *tile), f32),
            pltpu.VMEM((64, *tile), f32),
            pltpu.VMEM((64, *tile), f32),
            pltpu.VMEM((3, 16, *tile), f32),
            pltpu.VMEM((16, *tile), f32),
            pltpu.VMEM((15, *tile), f32),
            pltpu.VMEM((4, *tile), f32),
            pltpu.VMEM((16, *tile), f32),
            pltpu.VMEM((16, *tile), f32),
            sem((2, 2)), sem((2, 2)), sem((3, 2)), sem((15, 2)), sem((3, 2)), sem((15, 2)), sem((15, 2)),
        ],
        compiler_params=pltpu.CompilerParams(
            collective_id=0, has_side_effects=True, vmem_limit_bytes=40 * 1024 * 1024
        ),
        name="exchange",
    )(own, left_rim, right_rim, probe_sum)


def shards(object_slices, probe, mid_waves, amplitudes, row_offsets, col_offsets):
    count = lax.axis_size("tile")
    left = lax.ppermute(object_slices, "tile", [(i, i + 1) for i in range(count - 1)])
    right = lax.ppermute(object_slices, "tile", [(i + 1, i) for i in range(count - 1)])
    own, left_rim, right_rim, grad_probe = compute(
        object_slices, left, right, probe.reshape(2, 2, PX, PX), mid_waves[0, 0], amplitudes[0, 0],
        row_offsets[0, 0], col_offsets[0, 0],
    )
    total, shard, squares = exchange(own, left_rim, right_rim, grad_probe.reshape(4 * PX, PX))
    object_mean = jnp.sum(squares[0]) / (4 * object_slices.shape[1] * object_slices.shape[2] * 256)
    probe_mean = jnp.sum(squares[4]) / (4 * PX * PX)
    object_new = object_slices.astype(f32) - total * (object_step / jnp.sqrt(object_mean + epsilon))
    start = lax.axis_index("tile") * 16
    probe_rows = lax.dynamic_slice_in_dim(probe, start, 16, 0)
    probe_new = probe_rows - shard * (probe_step / jnp.sqrt(probe_mean + epsilon))
    return (object_new, probe_new)


def solution(mesh):
    return jax.shard_map(
        shards,
        mesh=mesh,
        in_specs=(
            P(None, "group", "tile"),
            P(),
            P("group", "tile", None, None, None, None, None),
            P("group", "tile", None, None, None),
            P("group", "tile", None),
            P("group", "tile", None),
        ),
        out_specs=(P(None, "group", "tile"), P("tile", None)),
        check_vma=False,
    )
```

time: 653 us -> 153 us (0.23); the launches traced: 642 us -> 153 us
  waiting for transfers between devices: 289 us -> 13.3 us
  matrix products: 165 us -> 0 us
  Pallas kernels: 0 us -> 124 us
  blocking collectives: 77.5 us -> 0 us
  local copies, waits for them, and re-layouts: 48.4 us -> 5.7 us
  between operations: 28.3 us -> 2.06 us
  other arithmetic: 19.1 us -> 3.01 us
  starting transfers between devices: 15.2 us -> 5.35 us
    psum x1 -> x0, waiting for transfers between devices: 289 us -> none  [shards(): probe_total = lax.psum(flat_probe, ('group', 'tile'))]
    dot_general x96 -> x0, matrix products: 165 us -> none  [the longest x12 22.9 us: spectral(): jnp.matmul(left_imag, signed, precision=highest)]
    pallas_call x0 -> x2, Pallas kernels: none -> 124 us  [the longest x1 98.1 us: exchange(): pl.pallas_call(exchange_kernel, out_shape=[jax.ShapeDtypeStruct(strip, f3...]
    psum x1 -> x0, blocking collectives: 77.5 us -> none  [shards(): object_total = lax.psum(object_squares, ('group', 'tile'))]
    dynamic_update_slice x3 -> x0, local copies, waits for them, and re-layouts: 41.6 us -> none  [shards(): lax.dynamic_update_slice(grad_obj, previous + update, (anchor, row_at, co...]
    ppermute x4 -> x2, waiting for transfers between devices: 0.01 us -> 13.3 us  [the longest x1 9.55 us: shards(): lax.ppermute(object_slices, 'tile', [(i, i + 1) for i in range(count - 1)])]
    ppermute x4 -> x2, starting transfers between devices: 15.1 us -> 5.35 us  [the longest x1 4.06 us: shards(): lax.ppermute(object_slices, 'tile', [(i, i + 1) for i in range(count - 1)])]
  transfers between devices with their start and end apart: 5 -> 2, of which waited for: 1 -> 2; matrix products, arithmetic and copies ran while one was open for 1% -> 0% of each run, Pallas kernels for 0% -> 0%
where the time goes in v1:
time: 153 us
  Pallas kernels  124 us (81%)
  waiting for transfers between devices  13.3 us (9%)
  local copies, waits for them, and re-layouts  5.7 us (4%)
  starting transfers between devices  5.35 us (3%)
  other arithmetic  3.01 us (2%)
  between operations  2.06 us (1%)
    pallas_call x1, Pallas kernels, exchange(): pl.pallas_call(exchange_kernel, out_shape=[jax.ShapeDtypeStruct(strip, f3...  98.1 us
    pallas_call x1, Pallas kernels, compute(): pl.pallas_call(compute_kernel, out_shape=[strip, strip, strip, jax.ShapeD...  25.7 us
    ppermute x1, waiting for transfers between devices, shards(): lax.ppermute(object_slices, 'tile', [(i, i + 1) for i in range(count - 1)])  9.55 us
    unnamed x14, local copies, waits for them, and re-layouts  5.7 us
    ppermute x1, starting transfers between devices, shards(): lax.ppermute(object_slices, 'tile', [(i, i + 1) for i in range(count - 1)])  4.06 us
    ppermute x1, waiting for transfers between devices, shards(): lax.ppermute(object_slices, 'tile', [(i + 1, i) for i in range(count - 1)])  3.72 us
  transfers between devices with their start and end apart: 2, of which 2 were waited for; matrix products, arithmetic and copies ran while one was open for 0% of the time, Pallas kernels for 0%

profile of v1, /device:TPU:1, one launch (start us, length us, event | category | flops | bytes accessed | tf_op | source)
XLA Modules:
  0.0 153.1 jit_solution(3168254687883587020)
XLA Ops:
  0.6 4.1 %collective-permute-start = (bf16[4,512,128]{2,1,0:T(8,128)(2,1)}, bf16[4,512,128]{2,1,0:T(8,128)(2,1)S(1)}, u32[]{:S(2)}, u32[]{:S(2)}) collective-permute-start(bf16[4,512,128]{2,1,0:T(8,128)(2,1)} %mid_obj.1), channel_id=1, source_target_pairs={{0,1},{1,2},{2,3},{3,4},{4,5},{5,6},{6,7},{7,8},{8,9},{9,10},{10,1... | collective-permute-start | bytes 1572872 | tf_op jit(solution)/shard_map/ppermute | solution.py:363
  4.7 1.3 collective-permute-start.1
  6.0 9.6 %collective-permute-done.left_obj = bf16[4,512,128]{2,1,0:T(8,128)(2,1)S(1)} collective-permute-done((bf16[4,512,128]{2,1,0:T(8,128)(2,1)}, bf16[4,512,128]{2,1,0:T(8,128)(2,1)S(1)}, u32[]{:S(2)}, u32[]{:S(2)}) %collective-permute-start) | collective-permute-done | bytes 524320 | tf_op jit(solution)/shard_map/ppermute | solution.py:363
  15.6 0.0 copy-start.5
  15.6 3.7 %collective-permute-done.1.right_obj = bf16[4,512,128]{2,1,0:T(8,128)(2,1)S(1)} collective-permute-done((bf16[4,512,128]{2,1,0:T(8,128)(2,1)}, bf16[4,512,128]{2,1,0:T(8,128)(2,1)S(1)}, u32[]{:S(2)}, u32[]{:S(2)}) %collective-permute-start.1) | collective-permute-done | bytes 524320 | tf_op jit(solution)/shard_map/ppermute | solution.py:364
  19.3 0.0 copy-start.6
  19.3 0.0 copy-done.5
  19.3 0.8 copy-done.6
  20.1 0.0 copy-start.4
  20.1 25.7 %gradient.1 = (f32[4,512,128]{2,1,0:T(8,128)}, f32[4,512,128]{2,1,0:T(8,128)}, f32[4,512,128]{2,1,0:T(8,128)}, f32[2,2,256,256]{3,2,1,0:T(8,128)}) custom-call(s32[3]{0:T(128)} %bitcast.10, s32[3]{0:T(128)} %bitcast.11, bf16[4,512,128]{2,1,0:T(8,128)(2,1)} %mid_obj.1, bf16[4,512,128]{2,1,0:T(8,128)(2,1)} %copy-done.5, bf16[4,512,128]{2,1,0:T(8,128)(2,1)} %copy-done.6, ...), custom_call_target="tpu_custom_call" | custom-call | tf_op jit(solution)/shard_map/gradient/pallas_call | solution.py:204
  45.7 0.0 copy-start
  45.7 1.2 copy-done
  47.0 0.0 copy-start.1
  47.0 1.2 copy-done.1
  48.2 0.0 copy-start.2
  48.2 1.2 copy-done.2
  49.4 0.0 copy-start.3
  49.4 1.2 copy-done.3
  50.6 98.1 %exchange.1 = (f32[4,512,128]{2,1,0:T(8,128)S(1)}, f32[16,256]{1,0:T(8,128)S(1)}, f32[8,128]{1,0:T(8,128)S(1)}) custom-call(f32[4,512,128]{2,1,0:T(8,128)S(1)} %copy-done, f32[4,512,128]{2,1,0:T(8,128)S(1)} %copy-done.1, f32[4,512,128]{2,1,0:T(8,128)S(1)} %copy-done.2, f32[1024,256]{1,0:T(8,128)S(1)} %bitcast.6), custom_call_target="tpu_custom_call" | custom-call | tf_op jit(solution)/shard_map/exchange/pallas_call | solution.py:329
  148.7 0.6 slice_reduce_fusion
  150.7 0.0 copy-done.4
  150.7 1.1 multiply_subtract_fusion
  151.8 1.3 multiply_subtract_fusion.1
Async XLA Ops:
  0.6 14.9 %collective-permute-start = (bf16[4,512,128]{2,1,0:T(8,128)(2,1)}, bf16[4,512,128]{2,1,0:T(8,128)(2,1)S(1)}, u32[]{:S(2)}, u32[]{:S(2)}) collective-permute-start(bf16[4,512,128]{2,1,0:T(8,128)(2,1)} %mid_obj.1), channel_id=1, source_target_pairs={{0,1},{1,2},{2,3},{3,4},{4,5},{5,6},{6,7},{7,8},{8,9},{9,10},{10,1... | collective-permute-start | bytes 1572872 | tf_op jit(solution)/shard_map/ppermute | solution.py:363
  4.7 14.6 %collective-permute-start.1 = (bf16[4,512,128]{2,1,0:T(8,128)(2,1)}, bf16[4,512,128]{2,1,0:T(8,128)(2,1)S(1)}, u32[]{:S(2)}, u32[]{:S(2)}) collective-permute-start(bf16[4,512,128]{2,1,0:T(8,128)(2,1)} %mid_obj.1), channel_id=1, source_target_pairs={{1,0},{2,1},{3,2},{4,3},{5,4},{6,5},{7,6},{8,7},{9,8},{10,9},{11,1... | collective-permute-start | bytes 1572872 | tf_op jit(solution)/shard_map/ppermute | solution.py:364
  15.6 3.7 %copy-start.5 = (bf16[4,512,128]{2,1,0:T(8,128)(2,1)}, bf16[4,512,128]{2,1,0:T(8,128)(2,1)S(1)}, u32[]{:S(2)}) copy-start(bf16[4,512,128]{2,1,0:T(8,128)(2,1)S(1)} %collective-permute-done.left_obj) | copy-start | bytes 1572868
  19.3 0.8 copy-start.6
  20.1 130.6 %copy-start.4 = (bf16[4,512,128]{2,1,0:T(8,128)(2,1)S(1)}, bf16[4,512,128]{2,1,0:T(8,128)(2,1)}, u32[]{:S(2)}) copy-start(bf16[4,512,128]{2,1,0:T(8,128)(2,1)} %mid_obj.1) | copy-start | bytes 1572868
  45.7 1.2 copy-start
  47.0 1.2 copy-start.1
  48.2 1.2 copy-start.2
  49.4 1.2 copy-start.3

commit v2 on v1

v2 whole, which is shorter than its diff:
```python
import numpy as np
import ml_dtypes
import jax
import jax.numpy as jnp
from jax import lax
from jax.sharding import PartitionSpec as P
from jax.experimental import pallas as pl
from jax.experimental.pallas import tpu as pltpu

phase_rate = 0.25
floor_level = 0.5
object_step = 0.5
probe_step = 0.5
epsilon = 1e-06
f32 = jnp.float32
bf16 = jnp.bfloat16
PX = 256
HALF = 128
TALL = PX + 8
ROWS = 512
POSITIONS = 3
CHUNKS = 8
LEVELS = 32767.0
OBJECT_COUNT = 4 * 2048 * 8192
PROBE_COUNT = 4 * PX * PX


def right_form(m):
    return np.block([[m.real, m.imag], [-m.imag, m.real]])


def left_form(m):
    return np.block([[m.real, -m.imag], [m.imag, m.real]])


def transform_tables():
    n = np.arange(HALF)[:, None]
    k = np.arange(HALF)[None, :]
    root = -2j * np.pi / PX
    even = np.exp(root * ((2 * n * k) % PX)) / np.sqrt(PX)
    odd = np.exp(root * ((n * (2 * k + 1)) % PX)) / np.sqrt(PX)
    freq = np.arange(PX)
    freq = np.where(freq < HALF, freq, freq - PX)
    phase = np.exp(2j * np.pi * phase_rate * freq * freq / PX)
    ring = np.fft.ifft(phase)
    i, j = np.meshgrid(np.arange(HALF), np.arange(HALF), indexing="ij")
    near, far = ring[(i - j) % PX], ring[(i - j + HALF) % PX]
    plus, minus = (near + far) / 2, (near - far) / 2
    forms = [
        right_form(even), right_form(odd),
        left_form(even.T), left_form(odd.T),
        left_form(even.conj()), left_form(odd.conj()),
        right_form(even.conj().T), right_form(odd.conj().T),
        right_form(plus.T), right_form(minus.T),
        left_form(plus), left_form(minus),
    ]
    whole = np.stack(forms)
    high = whole.astype(ml_dtypes.bfloat16)
    low = (whole - high.astype(np.float64)).astype(ml_dtypes.bfloat16)
    return np.stack([high, low], axis=1)


def split(x):
    high = x.astype(bf16)
    return high, (x - high.astype(f32)).astype(bf16)


def by_right(x, tables, index):
    high, low = split(x)
    t = tables[index, 0]
    return jnp.dot(
        jnp.concatenate([high, low, high], axis=1),
        jnp.concatenate([t, t, tables[index, 1]], axis=0),
        preferred_element_type=f32,
    )


def by_left(x, tables, index):
    high, low = split(x)
    t = tables[index, 0]
    return jnp.dot(
        jnp.concatenate([t, t, tables[index, 1]], axis=1),
        jnp.concatenate([high, low, high], axis=0),
        preferred_element_type=f32,
    )


def lanes(a, b):
    return jnp.concatenate([a, b], axis=1)


def rows(a, b):
    return jnp.concatenate([a, b], axis=0)


def halves(re, im):
    return lanes(re[:, :HALF], im[:, :HALF]), lanes(re[:, HALF:], im[:, HALF:])


def quantised(values, codes, scales):
    for k in range(CHUNKS):
        part = values[k * 64 : (k + 1) * 64]
        top = jnp.maximum(jnp.max(jnp.abs(part), axis=0, keepdims=True), 1e-30)
        scales[k : k + 1] = top * (1.0 / LEVELS)
        codes[k * 64 : (k + 1) * 64] = jnp.round(part * (LEVELS / top)).astype(jnp.int32).astype(jnp.int16)


def restored(codes, scales, k):
    return codes[k * 64 : (k + 1) * 64].astype(jnp.int32).astype(f32) * scales[k : k + 1]


def kernel(row_ref, col_ref, own_obj, probe_hbm, waves_hbm, amps_hbm, tables_hbm,
           object_new, probe_new,
           probe, waves, amps, tables, halo, obj, grad, pad, patch, far, back, upd, sorted_amps, gp,
           out_codes, out_scales, in_codes, in_scales,
           r1, s1, r2, s2, r3, s3, r4, fin, q1, q2,
           load_sems, halo_sems, code_sems, scale_sems, pair_sems, sems3, sems4, sems5, sems6, sems7):
    g = lax.axis_index("group")
    t = lax.axis_index("tile")
    layer, core = g // 2, g % 2
    x, zy = t // 16, t % 16
    spot = x * 4 + g
    right = (g, (t + 1) % 64)
    left = (g, (t + 63) % 64)
    other_core = (layer * 2 + 1 - core, t)
    other_layer = ((1 - layer) * 2 + core, t)

    def along_x(j):
        return (g, (x + j) % 4 * 16 + zy)

    def along_zy(j):
        return (g, x * 16 + (zy + j) % 16)

    def along_group(j):
        return ((g + j) % 4, t)

    def along_spot(j):
        to = (spot + j) % 16
        return (to % 4, to // 4 * 16 + zy)

    loads = [
        pltpu.make_async_copy(src, dst, load_sems.at[i])
        for i, (src, dst) in enumerate(
            [(amps_hbm, amps), (waves_hbm, waves), (tables_hbm, tables), (probe_hbm, probe)]
        )
    ]
    for load in loads:
        load.start()
    barrier = pltpu.get_barrier_semaphore()
    partners = [right, left] + [along_zy(j) for j in range(1, 16)] + [along_spot(j) for j in range(1, 16)]
    for partner in partners:
        pl.semaphore_signal(barrier, inc=1, device_id=partner, device_id_type=pl.DeviceIdType.MESH)
    pl.semaphore_wait(barrier, len(partners))

    def send(src, dst, sems, device):
        copy = pltpu.make_async_remote_copy(
            src_ref=src, dst_ref=dst, send_sem=sems.at[0], recv_sem=sems.at[1],
            device_id=device, device_id_type=pl.DeviceIdType.MESH,
        )
        copy.start()
        return copy

    halo_copies = []
    for s in (1, 0):
        part = pl.ds(2 * s, 2)
        halo_copies.append([
            send(own_obj.at[part], halo.at[0, part], halo_sems.at[0, s], right),
            send(own_obj.at[part], halo.at[1, part], halo_sems.at[1, s], left),
        ])

    at_row = lax.broadcasted_iota(jnp.int32, (PX, PX), 0)
    at_col = lax.broadcasted_iota(jnp.int32, (PX, PX), 1)
    sort_row = (at_col == jnp.where(at_row < HALF, 2 * at_row, 2 * at_row - PX + 1)).astype(f32).astype(bf16)
    sort_col = (at_row == jnp.where(at_col < HALF, 2 * at_col, 2 * at_col - PX + 1)).astype(f32).astype(bf16)
    grad[...] = jnp.zeros_like(grad)
    pad[:, :PX] = jnp.zeros((2, PX, 3 * HALF), f32)
    pad[:, PX + TALL :] = jnp.zeros((2, PX - 8, 3 * HALF), f32)
    obj[:, ROWS:, :] = jnp.zeros((2, 8, 3 * HALF), f32)
    gp[...] = jnp.zeros_like(gp)
    loads[0].wait()

    def sort_amps(p, carry):
        amp = jnp.dot(sort_row, amps[p], preferred_element_type=f32).astype(bf16)
        sorted_amps[p] = jnp.dot(amp, sort_col, preferred_element_type=f32)
        return carry

    lax.fori_loop(0, POSITIONS, sort_amps, 0)
    has_left = jnp.where(t > 0, 1.0, 0.0)
    has_right = jnp.where(t < 63, 1.0, 0.0)

    def widen(first):
        for c in range(2):
            obj[c, :ROWS, :HALF] = halo[0, first + c].astype(f32) * has_left
            obj[c, :ROWS, HALF : 2 * HALF] = own_obj[first + c].astype(f32)
            obj[c, :ROWS, 2 * HALF :] = halo[1, first + c].astype(f32) * has_right

    def offsets(p):
        row_at = row_ref[p]
        return lax.div(row_at, 8), lax.rem(row_at, 8), col_ref[p]

    def take_patch(p, dst):
        row_tile, row_rest, col_at = offsets(p)
        pick = (
            lax.broadcasted_iota(jnp.int32, (3 * HALF, PX), 0)
            == lax.broadcasted_iota(jnp.int32, (3 * HALF, PX), 1) + col_at
        ).astype(f32).astype(bf16)
        for c in range(2):
            raw = obj[c, pl.ds(row_tile * 8, TALL), :].astype(bf16)
            wide = jnp.dot(raw, pick, preferred_element_type=f32)
            dst[c] = pltpu.roll(wide, TALL - row_rest, 0)[:PX]

    def add_patch(p, first, values):
        row_tile, row_rest, col_at = offsets(p)
        place = (
            lax.broadcasted_iota(jnp.int32, (PX, 3 * HALF), 1)
            == lax.broadcasted_iota(jnp.int32, (PX, 3 * HALF), 0) + col_at
        ).astype(f32).astype(bf16)
        for c in range(2):
            high, low = split(values[c])
            moved = jnp.dot(lanes(high, low), rows(place, place), preferred_element_type=f32)
            moved = rows(moved, jnp.zeros((TALL - PX, 3 * HALF), f32))
            pad[c, PX : PX + TALL] = pltpu.roll(moved, row_rest, 0)
            grad[first + c] = grad[first + c] + pad[c, pl.ds((PX // 8 - row_tile) * 8, ROWS), :]

    def send_rims(first):
        copies = []
        for side, device in ((0, left), (1, right)):
            for c in range(2):
                quantised(
                    grad[first + c, :, side * 2 * HALF : side * 2 * HALF + HALF],
                    out_codes.at[side, first + c], out_scales.at[side, first + c],
                )
            part = pl.ds(first, 2)
            copies.append(send(out_codes.at[side, part], in_codes.at[side, part], code_sems.at[side, first // 2], device))
            copies.append(send(out_scales.at[side, part], in_scales.at[side, part], scale_sems.at[side, first // 2], device))
        return copies

    for load in loads[1:]:
        load.wait()
    for copy in halo_copies[0]:
        copy.wait()
    widen(2)

    def phase_one(p, carry):
        take_patch(p, patch)
        for m in range(2):
            sr, si = patch[0], patch[1]
            wr, wi = waves[p, 0, m].astype(f32), waves[p, 1, m].astype(f32)
            p0, p1 = halves(wr * sr - wi * si, wr * si + wi * sr)
            ye = by_right(p0 + p1, tables, 0)
            yo = by_right(p0 - p1, tables, 1)
            re = lanes(ye[:, :HALF], yo[:, :HALF])
            im = lanes(ye[:, HALF:], yo[:, HALF:])
            far[m, 0] = by_left(rows(re[:HALF] + re[HALF:], im[:HALF] + im[HALF:]), tables, 2)
            far[m, 1] = by_left(rows(re[:HALF] - re[HALF:], im[:HALF] - im[HALF:]), tables, 3)
        for e in range(2):
            power = 0.0
            for m in range(2):
                z = far[m, e]
                power = power + z[:HALF] * z[:HALF] + z[HALF:] * z[HALF:]
            factor = 1.0 - sorted_amps[p, e * HALF : (e + 1) * HALF] * jnp.minimum(
                lax.rsqrt(power), 1.0 / floor_level
            )
            factor = rows(factor, factor)
            for m in range(2):
                far[m, e] = far[m, e] * factor
        for m in range(2):
            u = by_left(far[m, 0], tables, 4)
            v = by_left(far[m, 1], tables, 5)
            s, d = u + v, u - v
            ie, io = halves(rows(s[:HALF], d[:HALF]), rows(s[HALF:], d[HALF:]))
            u = by_right(ie, tables, 6)
            v = by_right(io, tables, 7)
            s, d = u + v, u - v
            cr = lanes(s[:, :HALF], d[:, :HALF])
            ci = lanes(s[:, HALF:], d[:, HALF:])
            sr, si = patch[0], patch[1]
            wr, wi = waves[p, 0, m].astype(f32), waves[p, 1, m].astype(f32)
            gr, gi = wr * cr + wi * ci, wr * ci - wi * cr
            if m == 0:
                upd[p, 0], upd[p, 1] = gr, gi
            else:
                upd[p, 0], upd[p, 1] = upd[p, 0] + gr, upd[p, 1] + gi
            back[p, m, 0] = sr * cr + si * ci
            back[p, m, 1] = sr * ci - si * cr
        add_patch(p, 2, upd.at[p])
        return carry

    lax.fori_loop(0, POSITIONS, phase_one, 0)
    rim_two = send_rims(2)
    for copy in halo_copies[1]:
        copy.wait()
    widen(0)

    def phase_two(p, m):
        if m == 0:
            take_patch(p, upd.at[p])
        p0, p1 = halves(back[p, m, 0], back[p, m, 1])
        u = by_right(p0 + p1, tables, 8)
        v = by_right(p0 - p1, tables, 9)
        s, d = u + v, u - v
        re = lanes(s[:, :HALF], d[:, :HALF])
        im = lanes(s[:, HALF:], d[:, HALF:])
        u = by_left(rows(re[:HALF] + re[HALF:], im[:HALF] + im[HALF:]), tables, 10)
        v = by_left(rows(re[:HALF] - re[HALF:], im[:HALF] - im[HALF:]), tables, 11)
        s, d = u + v, u - v
        br = rows(s[:HALF], d[:HALF])
        bi = rows(s[HALF:], d[HALF:])
        pr, pi = probe[0, m], probe[1, m]
        ar, ai = upd[p, 0], upd[p, 1]
        gr, gi = pr * br + pi * bi, pr * bi - pi * br
        for part, value in enumerate((ar * br + ai * bi, ar * bi - ai * br)):
            for h in range(2):
                half = value[:, h * HALF : (h + 1) * HALF].reshape(16, 2, 8, HALF)
                gp[m, h, part] = gp[m, h, part] + half
        if m == 0:
            back[p, 0, 0], back[p, 0, 1] = gr, gi
        else:
            patch[0], patch[1] = back[p, 0, 0] + gr, back[p, 0, 1] + gi
            add_patch(p, 0, patch)

    def first_mode(p, carry):
        phase_two(p, 0)
        return carry

    def second_mode(p, carry):
        phase_two(p, 1)
        return carry

    def stage_one(m):
        return [send(gp.at[m, 1 - core], r1.at[m], pair_sems.at[0, m], other_core)]

    def stage_two(m):
        for l in range(2):
            s1[m, l] = gp[m, core, :, :, l] + r1[m, :, :, l]
        return [send(s1.at[m, 1 - layer], r2.at[m], pair_sems.at[1, m], other_layer)]

    def finish(copies):
        for copy in copies:
            copy.wait()

    lax.fori_loop(0, POSITIONS, first_mode, 0)
    one_a = stage_one(0)
    lax.fori_loop(0, 1, second_mode, 0)
    finish(one_a)
    two_a = stage_two(0)
    lax.fori_loop(1, POSITIONS, second_mode, 0)
    one_b = stage_one(1)
    rim_one = send_rims(0)
    finish(two_a)
    finish(one_b)
    two_b = stage_two(1)
    finish(rim_two)
    acc = jnp.zeros((8, HALF), f32)

    def total_of(c, acc):
        for k in range(CHUNKS):
            part = pl.ds(k * 64, 64)
            total = grad[c, part, HALF : 2 * HALF]
            total = total + restored(in_codes.at[0, c], in_scales.at[0, c], k) * has_right
            total = total + restored(in_codes.at[1, c], in_scales.at[1, c], k) * has_left
            object_new[c, part] = total
            acc = acc + jnp.sum((total * total).reshape(8, 8, HALF), axis=0)
        return acc

    for c in (2, 3):
        acc = total_of(c, acc)
    finish(two_b)
    for m in range(2):
        for part in range(2):
            s2[part * 2 + m] = s1[m, layer, part] + r2[m, part]
    copies = []
    for j in range(1, 4):
        copies.append(send(s2.at[(x + j) % 4], r3.at[j - 1], sems3.at[j - 1], along_x(j)))
    finish(copies)
    s3[...] = s2[x] + r3[0] + r3[1] + r3[2]
    four = [send(s3.at[(zy + j) % 16], r4.at[j - 1], sems4.at[j - 1], along_zy(j)) for j in range(1, 16)]
    finish(rim_one)
    for c in (0, 1):
        acc = total_of(c, acc)
    finish(four)
    piece = s3[zy]
    for j in range(15):
        piece = piece + r4[j]
    fin[0] = piece
    gathers = [send(fin.at[0], fin.at[j], sems5.at[j - 1], along_group(j)) for j in range(1, 4)]
    object_row = jnp.sum(acc, axis=0, keepdims=True)
    probe_row = jnp.sum(piece * piece, axis=0, keepdims=True)
    top = lax.broadcasted_iota(jnp.int32, (8, HALF), 0) < 4
    q1[0] = jnp.where(top, object_row, probe_row)
    finish([send(q1.at[0], q1.at[j], sems6.at[j - 1], along_zy(j)) for j in range(1, 16)])
    both = q1[zy]
    for s in range(1, 16):
        both = both + q1[(zy + 16 - s) % 16]
    q2[0] = both
    finish([send(q2.at[0], q2.at[j], sems7.at[j - 1], along_spot(j)) for j in range(1, 16)])
    both = q2[spot]
    for s in range(1, 16):
        both = both + q2[(spot + 16 - s) % 16]
    squares = jnp.sum(both, axis=1, keepdims=True)
    object_step_size = object_step * lax.rsqrt(squares[0:1] * (1.0 / OBJECT_COUNT) + epsilon)
    probe_step_size = probe_step * lax.rsqrt(squares[4:5] * (1.0 / PROBE_COUNT) + epsilon)
    for c in range(4):
        object_new[c] = own_obj[c].astype(f32) - object_new[c] * object_step_size
    finish(gathers)
    old = probe.at[x // 2, x % 2]
    for s in range(4):
        part = old[pl.ds(pl.multiple_of(zy * 16 + s // 2 * 8, 8), 8), s % 2 * HALF : s % 2 * HALF + HALF]
        probe_new[s // 2 * 8 : s // 2 * 8 + 8, s % 2 * HALF : s % 2 * HALF + HALF] = (
            part - fin[(g + 4 - s) % 4] * probe_step_size
        )


def shards(object_slices, probe, mid_waves, amplitudes, row_offsets, col_offsets):
    tables = jnp.asarray(transform_tables())
    tile = (8, HALF)
    whole = (PX, PX)
    vmem = pl.BlockSpec(memory_space=pltpu.VMEM)
    smem = pl.BlockSpec(memory_space=pltpu.SMEM)
    anywhere = pl.BlockSpec(memory_space=pl.ANY)
    sem = pltpu.SemaphoreType.DMA
    return pl.pallas_call(
        kernel,
        out_shape=[
            jax.ShapeDtypeStruct(object_slices.shape, f32),
            jax.ShapeDtypeStruct((16, PX), f32),
        ],
        in_specs=[smem, smem, vmem] + [anywhere] * 4,
        out_specs=[vmem] * 2,
        scratch_shapes=[
            pltpu.VMEM((2, 2, *whole), f32),
            pltpu.VMEM((3, 2, 2, *whole), bf16),
            pltpu.VMEM((3, *whole), bf16),
            pltpu.VMEM(tables.shape, bf16),
            pltpu.VMEM((2, 4, ROWS, HALF), bf16),
            pltpu.VMEM((2, ROWS + 8, 3 * HALF), f32),
            pltpu.VMEM((4, ROWS, 3 * HALF), f32),
            pltpu.VMEM((2, ROWS + PX, 3 * HALF), f32),
            pltpu.VMEM((2, *whole), f32),
            pltpu.VMEM((2, 2, *whole), f32),
            pltpu.VMEM((3, 2, 2, *whole), f32),
            pltpu.VMEM((3, 2, *whole), f32),
            pltpu.VMEM((3, *whole), f32),
            pltpu.VMEM((2, 2, 2, 16, 2, *tile), f32),
            pltpu.VMEM((2, 4, ROWS, HALF), jnp.int16),
            pltpu.VMEM((2, 4, *tile), f32),
            pltpu.VMEM((2, 4, ROWS, HALF), jnp.int16),
            pltpu.VMEM((2, 4, *tile), f32),
            pltpu.VMEM((2, 2, 16, 2, *tile), f32),
            pltpu.VMEM((2, 2, 2, 16, *tile), f32),
            pltpu.VMEM((2, 2, 16, *tile), f32),
            pltpu.VMEM((4, 16, *tile), f32),
            pltpu.VMEM((3, 16, *tile), f32),
            pltpu.VMEM((16, *tile), f32),
            pltpu.VMEM((15, *tile), f32),
            pltpu.VMEM((4, *tile), f32),
            pltpu.VMEM((16, *tile), f32),
            pltpu.VMEM((16, *tile), f32),
            sem((4,)), sem((2, 2, 2)), sem((2, 2, 2)), sem((2, 2, 2)), sem((2, 2, 2)),
            sem((3, 2)), sem((15, 2)), sem((3, 2)), sem((15, 2)), sem((15, 2)),
        ],
        compiler_params=pltpu.CompilerParams(
            collective_id=0, has_side_effects=True, vmem_limit_bytes=56 * 1024 * 1024
        ),
        name="update",
    )(
        row_offsets[0, 0], col_offsets[0, 0], object_slices, probe.reshape(2, 2, *whole),
        mid_waves[0, 0], amplitudes[0, 0], tables,
    )


def solution(mesh):
    return jax.shard_map(
        shards,
        mesh=mesh,
        in_specs=(
            P(None, "group", "tile"),
            P(),
            P("group", "tile", None, None, None, None, None),
            P("group", "tile", None, None, None),
            P("group", "tile", None),
            P("group", "tile", None),
        ),
        out_specs=(P(None, "group", "tile"), P("tile", None)),
        check_vma=False,
    )
```

time: 153 us -> 99.1 us (0.65)
  Pallas kernels: 124 us -> 94.7 us
  waiting for transfers between devices: 13.3 us -> 0 us
  starting transfers between devices: 5.35 us -> 0 us
  other arithmetic: 3.01 us -> 0 us
  local copies, waits for them, and re-layouts: 5.7 us -> 3.59 us
    pallas_call x2 -> x1, Pallas kernels: 124 us -> 94.7 us  [shards(): pl.pallas_call(kernel, out_shape=[jax.ShapeDtypeStruct(object_slices.shap...]
    ppermute x2 -> x0, waiting for transfers between devices: 13.3 us -> none  [the longest x1 9.55 us: shards(): lax.ppermute(object_slices, 'tile', [(i, i + 1) for i in range(count - 1)])]
    ppermute x2 -> x0, starting transfers between devices: 5.35 us -> none  [the longest x1 4.06 us: shards(): lax.ppermute(object_slices, 'tile', [(i, i + 1) for i in range(count - 1)])]
    sub x2 -> x0, other arithmetic: 2.4 us -> none  [the longest x1 1.33 us: shards(): probe_rows - shard * (probe_step / jnp.sqrt(probe_mean + epsilon))]
    unnamed x14 -> x2, local copies, waits for them, and re-layouts: 5.7 us -> 3.59 us
  transfers between devices with their start and end apart: 2 -> 0, of which waited for: 2 -> 0; matrix products, arithmetic and copies ran while one was open for 0% -> 0% of each run, Pallas kernels for 0% -> 0%
where the time goes in v2:
time: 99.1 us; the launch traced here: 98.9 us
  Pallas kernels  94.7 us (96%)
  local copies, waits for them, and re-layouts  3.59 us (4%)
    pallas_call x1, Pallas kernels, shards(): pl.pallas_call(kernel, out_shape=[jax.ShapeDtypeStruct(object_slices.shap...  94.7 us
    unnamed x2, local copies, waits for them, and re-layouts  3.59 us

profile of v2, /device:TPU:1, one launch (start us, length us, event | category | flops | bytes accessed | tf_op | source)
XLA Modules:
  0.0 98.9 jit_solution(7669126690968360936)
XLA Ops:
  0.6 94.7 %update.1 = (f32[4,512,128]{2,1,0:T(8,128)}, f32[16,256]{1,0:T(8,128)}) custom-call(s32[3]{0:T(128)} %bitcast.8, s32[3]{0:T(128)} %bitcast.9, bf16[4,512,128]{2,1,0:T(8,128)(2,1)} %own_obj.1, f32[2,2,256,256]{3,2,1,0:T(8,128)} %bitcast.6, bf16[3,2,2,256,256]{4,3,2,1,0:T(8,128)(2,1)} %bitcast.5, bf16[3,256,256]{2,1,0:T(8,128)(2,1)} %bitcast.7, ...), custom_call_target="tpu_custom_call" | custom-call | tf_op jit(solution)/shard_map/update/pallas_call | solution.py:422
  95.3 2.3 %copy.11 = f32[4,512,128]{2,1,0:T(8,128)} copy(f32[4,512,128]{2,1,0:T(8,128)} %get-tuple-element.4) | data formatting | bytes 2097152
  97.6 1.3 %copy.12 = f32[16,256]{1,0:T(8,128)} copy(f32[16,256]{1,0:T(8,128)} %get-tuple-element.5) | data formatting | bytes 32768

commit v3 on v2

--- a/solution.py
+++ b/solution.py
@@ -20,6 +20,8 @@
 ROWS = 512
 POSITIONS = 3
 CHUNKS = 8
+PIECES = 4
+CHUNK_ROWS = ROWS // PIECES
 LEVELS = 32767.0
 OBJECT_COUNT = 4 * 2048 * 8192
 PROBE_COUNT = 4 * PX * PX
@@ -110,11 +112,12 @@
 
 
 def kernel(row_ref, col_ref, own_obj, probe_hbm, waves_hbm, amps_hbm, tables_hbm,
-           object_new, probe_new,
+           total_out, squares_out, shard_out,
            probe, waves, amps, tables, halo, obj, grad, pad, patch, far, back, upd, sorted_amps, gp,
            out_codes, out_scales, in_codes, in_scales,
-           r1, s1, r2, s2, r3, s3, r4, fin, q1, q2,
-           load_sems, halo_sems, code_sems, scale_sems, pair_sems, sems3, sems4, sems5, sems6, sems7):
+           halo_relay, code_relay, r1, s1, r2, s2, r3, s3, r4, fin, q1, q2,
+           load_sems, direct_sems, chunk_sems, relay_sems, onward_sems, scale_sems, pair_sems,
+           sems3, sems4, sems5, sems6, sems7):
     g = lax.axis_index("group")
     t = lax.axis_index("tile")
     layer, core = g // 2, g % 2
@@ -122,6 +125,11 @@
     spot = x * 4 + g
     right = (g, (t + 1) % 64)
     left = (g, (t + 63) % 64)
+    y = zy % 4
+    onward = ((g, (t + 4) % 64), (g, (t + 60) % 64))
+    wrapped = ((g, t - y), (g, t - y + 3))
+    at_end = (y == 3, y == 0)
+    at_start = (y == 0, y == 3)
     other_core = (layer * 2 + 1 - core, t)
     other_layer = ((1 - layer) * 2 + core, t)
 
@@ -147,7 +155,7 @@
     for load in loads:
         load.start()
     barrier = pltpu.get_barrier_semaphore()
-    partners = [right, left] + [along_zy(j) for j in range(1, 16)] + [along_spot(j) for j in range(1, 16)]
+    partners = [right, left, *onward] + [along_zy(j) for j in range(1, 16)] + [along_spot(j) for j in range(1, 16)]
     for partner in partners:
         pl.semaphore_signal(barrier, inc=1, device_id=partner, device_id_type=pl.DeviceIdType.MESH)
     pl.semaphore_wait(barrier, len(partners))
@@ -160,13 +168,106 @@
         copy.start()
         return copy
 
-    halo_copies = []
-    for s in (1, 0):
-        part = pl.ds(2 * s, 2)
-        halo_copies.append([
-            send(own_obj.at[part], halo.at[0, part], halo_sems.at[0, s], right),
-            send(own_obj.at[part], halo.at[1, part], halo_sems.at[1, s], left),
-        ])
+    class Swap:
+        def __init__(self, number, src, dst, relay, first):
+            self.number, self.src, self.dst, self.relay, self.first = number, src, dst, relay, first
+
+        def near(self, side):
+            return right if side == 0 else left
+
+        def chunk(self, ref, k):
+            return ref.at[pl.ds(k * CHUNK_ROWS, CHUNK_ROWS)]
+
+        def copy(self, src, dst, send_sem, recv_sem, device):
+            return pltpu.make_async_remote_copy(
+                src_ref=src, dst_ref=dst, send_sem=send_sem, recv_sem=recv_sem,
+                device_id=device, device_id_type=pl.DeviceIdType.MESH,
+            )
+
+        def direct(self, side):
+            sems = direct_sems.at[self.number, side]
+            return self.copy(
+                self.src(side).at[self.first], self.dst(side).at[self.first], sems.at[0], sems.at[1], self.near(side)
+            )
+
+        def plain(self, side, k):
+            sems = chunk_sems.at[self.number, side, k]
+            second = self.first + 1
+            return self.copy(
+                self.chunk(self.src(side).at[second], k), self.chunk(self.dst(side).at[second], k),
+                sems.at[0], sems.at[1], self.near(side),
+            )
+
+        def detour(self, side, k):
+            sems = relay_sems.at[self.number, side, k]
+            return self.copy(
+                self.chunk(self.src(side).at[self.first + 1], k), self.chunk(self.relay(side), k),
+                sems.at[0], sems.at[1], wrapped[side],
+            )
+
+        def forwarded(self, side, k):
+            return self.copy(
+                self.chunk(self.relay(side), k), self.chunk(self.dst(side).at[self.first + 1], k),
+                onward_sems.at[self.number, side, k], chunk_sems.at[self.number, side, k].at[1], onward[side],
+            )
+
+        def start(self):
+            for side in range(2):
+                @pl.when(at_end[side])
+                def _():
+                    for k in range(PIECES):
+                        self.detour(side, k).start()
+
+                @pl.when(jnp.logical_not(at_end[side]))
+                def _():
+                    for k in range(PIECES):
+                        self.plain(side, k).start()
+
+            for side in range(2):
+                self.direct(side).start()
+
+        def forward(self):
+            for side in range(2):
+                @pl.when(at_start[side])
+                def _():
+                    for k in range(PIECES):
+                        self.detour(side, k).wait_recv()
+                        self.forwarded(side, k).start()
+
+        def wait(self):
+            for side in range(2):
+                for k in range(PIECES):
+                    self.plain(side, k).wait_recv()
+                self.direct(side).wait()
+
+                @pl.when(at_end[side])
+                def _():
+                    for k in range(PIECES):
+                        self.detour(side, k).wait_send()
+
+                @pl.when(jnp.logical_not(at_end[side]))
+                def _():
+                    for k in range(PIECES):
+                        self.plain(side, k).wait_send()
+
+                @pl.when(at_start[side])
+                def _():
+                    for k in range(PIECES):
+                        self.forwarded(side, k).wait_send()
+
+    def halo_swap(number, first):
+        return Swap(number, lambda side: own_obj, lambda side: halo.at[side], lambda side: halo_relay.at[number, side], first)
+
+    def rim_swap(number, first):
+        return Swap(
+            number, lambda side: out_codes.at[side], lambda side: in_codes.at[side],
+            lambda side: code_relay.at[number - 2, side], first,
+        )
+
+    halo_two, halo_one = halo_swap(0, 2), halo_swap(1, 0)
+    rim_two, rim_one = rim_swap(2, 2), rim_swap(3, 0)
+    halo_two.start()
+    halo_one.start()
 
     at_row = lax.broadcasted_iota(jnp.int32, (PX, PX), 0)
     at_col = lax.broadcasted_iota(jnp.int32, (PX, PX), 1)
@@ -222,23 +323,28 @@
             pad[c, PX : PX + TALL] = pltpu.roll(moved, row_rest, 0)
             grad[first + c] = grad[first + c] + pad[c, pl.ds((PX // 8 - row_tile) * 8, ROWS), :]
 
-    def send_rims(first):
+    def send_rims(swap):
+        first = swap.first
         copies = []
-        for side, device in ((0, left), (1, right)):
+        for side in range(2):
+            from_lane = 2 * HALF * (1 - side)
             for c in range(2):
                 quantised(
-                    grad[first + c, :, side * 2 * HALF : side * 2 * HALF + HALF],
+                    grad[first + c, :, from_lane : from_lane + HALF],
                     out_codes.at[side, first + c], out_scales.at[side, first + c],
                 )
+        swap.start()
+        for side in range(2):
             part = pl.ds(first, 2)
-            copies.append(send(out_codes.at[side, part], in_codes.at[side, part], code_sems.at[side, first // 2], device))
-            copies.append(send(out_scales.at[side, part], in_scales.at[side, part], scale_sems.at[side, first // 2], device))
+            copies.append(
+                send(out_scales.at[side, part], in_scales.at[side, part], scale_sems.at[side, first // 2], swap.near(side))
+            )
         return copies
 
     for load in loads[1:]:
         load.wait()
-    for copy in halo_copies[0]:
-        copy.wait()
+    halo_two.forward()
+    halo_two.wait()
     widen(2)
 
     def phase_one(p, carry):
@@ -284,12 +390,16 @@
             back[p, m, 0] = sr * cr + si * ci
             back[p, m, 1] = sr * ci - si * cr
         add_patch(p, 2, upd.at[p])
+
+        @pl.when(p == 1)
+        def _():
+            halo_one.forward()
+
         return carry
 
     lax.fori_loop(0, POSITIONS, phase_one, 0)
-    rim_two = send_rims(2)
-    for copy in halo_copies[1]:
-        copy.wait()
+    scale_two = send_rims(rim_two)
+    halo_one.wait()
     widen(0)
 
     def phase_two(p, m):
@@ -341,25 +451,28 @@
 
     lax.fori_loop(0, POSITIONS, first_mode, 0)
     one_a = stage_one(0)
+    rim_two.forward()
     lax.fori_loop(0, 1, second_mode, 0)
     finish(one_a)
     two_a = stage_two(0)
     lax.fori_loop(1, POSITIONS, second_mode, 0)
     one_b = stage_one(1)
-    rim_one = send_rims(0)
+    scale_one = send_rims(rim_one)
     finish(two_a)
     finish(one_b)
     two_b = stage_two(1)
-    finish(rim_two)
+    rim_two.wait()
+    finish(scale_two)
+    rim_one.forward()
     acc = jnp.zeros((8, HALF), f32)
 
     def total_of(c, acc):
         for k in range(CHUNKS):
             part = pl.ds(k * 64, 64)
             total = grad[c, part, HALF : 2 * HALF]
-            total = total + restored(in_codes.at[0, c], in_scales.at[0, c], k) * has_right
-            total = total + restored(in_codes.at[1, c], in_scales.at[1, c], k) * has_left
-            object_new[c, part] = total
+            total = total + restored(in_codes.at[1, c], in_scales.at[1, c], k) * has_right
+            total = total + restored(in_codes.at[0, c], in_scales.at[0, c], k) * has_left
+            total_out[c, part] = total
             acc = acc + jnp.sum((total * total).reshape(8, 8, HALF), axis=0)
         return acc
 
@@ -375,7 +488,8 @@
     finish(copies)
     s3[...] = s2[x] + r3[0] + r3[1] + r3[2]
     four = [send(s3.at[(zy + j) % 16], r4.at[j - 1], sems4.at[j - 1], along_zy(j)) for j in range(1, 16)]
-    finish(rim_one)
+    rim_one.wait()
+    finish(scale_one)
     for c in (0, 1):
         acc = total_of(c, acc)
     finish(four)
@@ -397,18 +511,20 @@
     both = q2[spot]
     for s in range(1, 16):
         both = both + q2[(spot + 16 - s) % 16]
-    squares = jnp.sum(both, axis=1, keepdims=True)
-    object_step_size = object_step * lax.rsqrt(squares[0:1] * (1.0 / OBJECT_COUNT) + epsilon)
-    probe_step_size = probe_step * lax.rsqrt(squares[4:5] * (1.0 / PROBE_COUNT) + epsilon)
+    squares_out[...] = both
+    finish(gathers)
+    for s in range(4):
+        shard_out[s // 2 * 8 : s // 2 * 8 + 8, s % 2 * HALF : s % 2 * HALF + HALF] = fin[(g + 4 - s) % 4]
+
+
+def final_kernel(own_obj, total, squares, shard, old_probe, object_new, probe_new):
+    sums = jnp.sum(squares[...], axis=1, keepdims=True)
+    object_step_size = object_step * lax.rsqrt(sums[0:1] * (1.0 / OBJECT_COUNT) + epsilon)
+    probe_step_size = probe_step * lax.rsqrt(sums[4:5] * (1.0 / PROBE_COUNT) + epsilon)
     for c in range(4):
-        object_new[c] = own_obj[c].astype(f32) - object_new[c] * object_step_size
-    finish(gathers)
-    old = probe.at[x // 2, x % 2]
-    for s in range(4):
-        part = old[pl.ds(pl.multiple_of(zy * 16 + s // 2 * 8, 8), 8), s % 2 * HALF : s % 2 * HALF + HALF]
-        probe_new[s // 2 * 8 : s // 2 * 8 + 8, s % 2 * HALF : s % 2 * HALF + HALF] = (
-            part - fin[(g + 4 - s) % 4] * probe_step_size
-        )
+        object_new[c] = own_obj[c].astype(f32) - total[c] * object_step_size
+    at = pl.multiple_of(lax.axis_index("tile") * 16, 16)
+    probe_new[...] = old_probe[pl.ds(at, 16), :] - shard[...] * probe_step_size
 
 
 def shards(object_slices, probe, mid_waves, amplitudes, row_offsets, col_offsets):
@@ -419,14 +535,13 @@
     smem = pl.BlockSpec(memory_space=pltpu.SMEM)
     anywhere = pl.BlockSpec(memory_space=pl.ANY)
     sem = pltpu.SemaphoreType.DMA
-    return pl.pallas_call(
+    strip = jax.ShapeDtypeStruct(object_slices.shape, f32)
+    shard = jax.ShapeDtypeStruct((16, PX), f32)
+    total, squares, shard_sum = pl.pallas_call(
         kernel,
-        out_shape=[
-            jax.ShapeDtypeStruct(object_slices.shape, f32),
-            jax.ShapeDtypeStruct((16, PX), f32),
-        ],
+        out_shape=[strip, jax.ShapeDtypeStruct(tile, f32), shard],
         in_specs=[smem, smem, vmem] + [anywhere] * 4,
-        out_specs=[vmem] * 2,
+        out_specs=[vmem] * 3,
         scratch_shapes=[
             pltpu.VMEM((2, 2, *whole), f32),
             pltpu.VMEM((3, 2, 2, *whole), bf16),
@@ -446,6 +561,8 @@
             pltpu.VMEM((2, 4, *tile), f32),
             pltpu.VMEM((2, 4, ROWS, HALF), jnp.int16),
             pltpu.VMEM((2, 4, *tile), f32),
+            pltpu.VMEM((2, 2, ROWS, HALF), bf16),
+            pltpu.VMEM((2, 2, ROWS, HALF), jnp.int16),
             pltpu.VMEM((2, 2, 16, 2, *tile), f32),
             pltpu.VMEM((2, 2, 2, 16, *tile), f32),
             pltpu.VMEM((2, 2, 16, *tile), f32),
@@ -456,7 +573,8 @@
             pltpu.VMEM((4, *tile), f32),
             pltpu.VMEM((16, *tile), f32),
             pltpu.VMEM((16, *tile), f32),
-            sem((4,)), sem((2, 2, 2)), sem((2, 2, 2)), sem((2, 2, 2)), sem((2, 2, 2)),
+            sem((4,)), sem((4, 2, 2)), sem((4, 2, PIECES, 2)), sem((4, 2, PIECES, 2)), sem((4, 2, PIECES)),
+            sem((2, 2, 2)), sem((2, 2, 2)),
             sem((3, 2)), sem((15, 2)), sem((3, 2)), sem((15, 2)), sem((15, 2)),
         ],
         compiler_params=pltpu.CompilerParams(
@@ -467,6 +585,14 @@
         row_offsets[0, 0], col_offsets[0, 0], object_slices, probe.reshape(2, 2, *whole),
         mid_waves[0, 0], amplitudes[0, 0], tables,
     )
+    return pl.pallas_call(
+        final_kernel,
+        out_shape=[strip, shard],
+        in_specs=[vmem] * 5,
+        out_specs=[vmem] * 2,
+        compiler_params=pltpu.CompilerParams(vmem_limit_bytes=16 * 1024 * 1024),
+        name="final",
+    )(object_slices, total, squares, shard_sum, probe)
 
 
 def solution(mesh):

time: 99.1 us -> 88.3 us (0.89)
  Pallas kernels: 94.7 us -> 84.8 us
    pallas_call x1 -> x2, Pallas kernels: 94.7 us -> 84.8 us  [the longest x1 83.6 us: shards(): pl.pallas_call(kernel, out_shape=[strip, jax.ShapeDtypeStruct(tile, f32),...]
    unnamed x2 -> x10, local copies, waits for them, and re-layouts: 3.59 us -> 2.62 us
where the time goes in v3:
time: 88.3 us; the launch traced here: 88.1 us
  Pallas kernels  84.8 us (96%)
  local copies, waits for them, and re-layouts  2.62 us (3%)
    pallas_call x1, Pallas kernels, shards(): pl.pallas_call(kernel, out_shape=[strip, jax.ShapeDtypeStruct(tile, f32),...  83.6 us
    unnamed x10, local copies, waits for them, and re-layouts  2.62 us

profile of v3, /device:TPU:1, one launch (start us, length us, event | category | flops | bytes accessed | tf_op | source)
XLA Modules:
  0.0 88.1 jit_solution(1407283749563076890)
XLA Ops:
  0.6 0.0 copy-start
  0.6 0.0 copy-start.1
  0.7 83.6 %update.1 = (f32[4,512,128]{2,1,0:T(8,128)}, f32[8,128]{1,0:T(8,128)}, f32[16,256]{1,0:T(8,128)}) custom-call(s32[3]{0:T(128)} %bitcast.8, s32[3]{0:T(128)} %bitcast.9, bf16[4,512,128]{2,1,0:T(8,128)(2,1)} %own_obj.3, f32[2,2,256,256]{3,2,1,0:T(8,128)} %bitcast.5, bf16[3,2,2,256,256]{4,3,2,1,0:T(8,128)(2,1)} %bitcast.6, bf16[3,256,256]{2,1,0:T(8,128)(2,1)} %bitcast.7, ...), custom_call_target="tpu_custom_call" | custom-call | tf_op jit(solution)/shard_map/update/pallas_call | solution.py:540
  84.2 0.0 copy-done
  84.2 0.0 copy-done.1
  84.3 0.0 copy-start.2
  84.3 1.2 %copy-done.2 = f32[4,512,128]{2,1,0:T(8,128)S(1)} copy-done((f32[4,512,128]{2,1,0:T(8,128)S(1)}, f32[4,512,128]{2,1,0:T(8,128)}, u32[]{:S(2)}) %copy-start.2) | copy-done | bytes 1048600
  85.5 0.0 copy-start.3
  85.5 0.7 copy-done.3
  86.2 0.0 copy-start.4
  86.2 0.7 copy-done.4
  86.9 1.2 %final.1 = (f32[4,512,128]{2,1,0:T(8,128)}, f32[16,256]{1,0:T(8,128)}) custom-call(bf16[4,512,128]{2,1,0:T(8,128)(2,1)S(1)} %copy-done.1, f32[4,512,128]{2,1,0:T(8,128)S(1)} %copy-done.2, f32[8,128]{1,0:T(8,128)S(1)} %copy-done.4, f32[16,256]{1,0:T(8,128)S(1)} %copy-done.3, f32[1024,256]{1,0:T(8,128)S(1)} %copy-done), custom_call_target="tpu_custom_call" | custom-call | tf_op jit(solution)/shard_map/final/pallas_call | solution.py:588
Async XLA Ops:
  0.6 83.6 %copy-start = (f32[1024,256]{1,0:T(8,128)S(1)}, f32[1024,256]{1,0:T(8,128)}, u32[]{:S(2)}) copy-start(f32[1024,256]{1,0:T(8,128)} %old_probe.1) | copy-start | bytes 3145732
  0.6 83.6 %copy-start.1 = (bf16[4,512,128]{2,1,0:T(8,128)(2,1)S(1)}, bf16[4,512,128]{2,1,0:T(8,128)(2,1)}, u32[]{:S(2)}) copy-start(bf16[4,512,128]{2,1,0:T(8,128)(2,1)} %own_obj.3) | copy-start | bytes 1572868
  84.3 1.2 %copy-start.2 = (f32[4,512,128]{2,1,0:T(8,128)S(1)}, f32[4,512,128]{2,1,0:T(8,128)}, u32[]{:S(2)}) copy-start(f32[4,512,128]{2,1,0:T(8,128)} %get-tuple-element.5.total) | copy-start | bytes 3145732
  85.5 0.7 copy-start.3
  86.2 0.7 copy-start.4

commit v4 on v3

--- a/solution.py
+++ b/solution.py
@@ -21,8 +21,10 @@
 POSITIONS = 3
 CHUNKS = 8
 PIECES = 4
+STEP = 32
 CHUNK_ROWS = ROWS // PIECES
 LEVELS = 32767.0
+LEVELS_TWO = 32000.0
 OBJECT_COUNT = 4 * 2048 * 8192
 PROBE_COUNT = 4 * PX * PX
 
@@ -67,24 +69,26 @@
     return high, (x - high.astype(f32)).astype(bf16)
 
 
-def by_right(x, tables, index):
-    high, low = split(x)
-    t = tables[index, 0]
+def by_right(high, low, tables, index):
+    h, t = high[...], tables[index, 0]
     return jnp.dot(
-        jnp.concatenate([high, low, high], axis=1),
+        jnp.concatenate([h, low[...], h], axis=1),
         jnp.concatenate([t, t, tables[index, 1]], axis=0),
         preferred_element_type=f32,
     )
 
 
-def by_left(x, tables, index):
-    high, low = split(x)
-    t = tables[index, 0]
+def by_left(high, low, tables, index):
+    h, t = high[...], tables[index, 0]
     return jnp.dot(
         jnp.concatenate([t, t, tables[index, 1]], axis=1),
-        jnp.concatenate([high, low, high], axis=0),
+        jnp.concatenate([h, low[...], h], axis=0),
         preferred_element_type=f32,
     )
+
+
+def put(high, low, at, value):
+    high[at : at + STEP], low[at : at + STEP] = split(value)
 
 
 def lanes(a, b):
@@ -113,14 +117,13 @@
 
 def kernel(row_ref, col_ref, own_obj, probe_hbm, waves_hbm, amps_hbm, tables_hbm,
            total_out, squares_out, shard_out,
-           probe, waves, amps, tables, halo, obj, grad, pad, patch, far, back, upd, sorted_amps, gp,
+           probe, waves, amps, tables, halo, obj, grad, pad, patch, far, back_high, back_low, highs, lows, products, upd, sorted_amps, gp,
            out_codes, out_scales, in_codes, in_scales,
-           halo_relay, code_relay, r1, s1, r2, s2, r3, s3, r4, fin, q1, q2,
-           load_sems, direct_sems, chunk_sems, relay_sems, onward_sems, scale_sems, pair_sems,
+           halo_relay, code_relay, probe_codes, r1, s3, r4, fin, q1, q2,
+           load_sems, direct_sems, chunk_sems, relay_sems, onward_sems, scale_sems,
            sems3, sems4, sems5, sems6, sems7):
     g = lax.axis_index("group")
     t = lax.axis_index("tile")
-    layer, core = g // 2, g % 2
     x, zy = t // 16, t % 16
     spot = x * 4 + g
     right = (g, (t + 1) % 64)
@@ -130,12 +133,6 @@
     wrapped = ((g, t - y), (g, t - y + 3))
     at_end = (y == 3, y == 0)
     at_start = (y == 0, y == 3)
-    other_core = (layer * 2 + 1 - core, t)
-    other_layer = ((1 - layer) * 2 + core, t)
-
-    def along_x(j):
-        return (g, (x + j) % 4 * 16 + zy)
-
     def along_zy(j):
         return (g, x * 16 + (zy + j) % 16)
 
@@ -267,7 +264,6 @@
     halo_two, halo_one = halo_swap(0, 2), halo_swap(1, 0)
     rim_two, rim_one = rim_swap(2, 2), rim_swap(3, 0)
     halo_two.start()
-    halo_one.start()
 
     at_row = lax.broadcasted_iota(jnp.int32, (PX, PX), 0)
     at_col = lax.broadcasted_iota(jnp.int32, (PX, PX), 1)
@@ -345,50 +341,78 @@
         load.wait()
     halo_two.forward()
     halo_two.wait()
+    halo_one.start()
     widen(2)
+
+    def stacked_halves(high, low, product, mixed):
+        for r in range(0, HALF, STEP):
+            for i in range(2):
+                here = pl.ds(r, STEP), slice(i * HALF, i * HALF + HALF)
+                there = pl.ds(HALF + r, STEP), slice(i * HALF, i * HALF + HALF)
+                u, v = product[0, here[0], here[1]], product[1, here[0], here[1]]
+                top = lanes(u + v, u - v) if mixed else lanes(u, v)
+                u, v = product[0, there[0], there[1]], product[1, there[0], there[1]]
+                bottom = lanes(u + v, u - v) if mixed else lanes(u, v)
+                put(high.at[0], low.at[0], i * HALF + r, top + bottom)
+                put(high.at[1], low.at[1], i * HALF + r, top - bottom)
 
     def phase_one(p, carry):
         take_patch(p, patch)
         for m in range(2):
-            sr, si = patch[0], patch[1]
-            wr, wi = waves[p, 0, m].astype(f32), waves[p, 1, m].astype(f32)
-            p0, p1 = halves(wr * sr - wi * si, wr * si + wi * sr)
-            ye = by_right(p0 + p1, tables, 0)
-            yo = by_right(p0 - p1, tables, 1)
-            re = lanes(ye[:, :HALF], yo[:, :HALF])
-            im = lanes(ye[:, HALF:], yo[:, HALF:])
-            far[m, 0] = by_left(rows(re[:HALF] + re[HALF:], im[:HALF] + im[HALF:]), tables, 2)
-            far[m, 1] = by_left(rows(re[:HALF] - re[HALF:], im[:HALF] - im[HALF:]), tables, 3)
+            high, low, product = highs.at[m], lows.at[m], products.at[m]
+            for r in range(0, PX, STEP):
+                part = pl.ds(r, STEP)
+                sr, si = patch[0, part], patch[1, part]
+                wr, wi = waves[p, 0, m, part].astype(f32), waves[p, 1, m, part].astype(f32)
+                p0, p1 = halves(wr * sr - wi * si, wr * si + wi * sr)
+                put(high.at[0], low.at[0], r, p0 + p1)
+                put(high.at[1], low.at[1], r, p0 - p1)
+            for e in range(2):
+                product[e] = by_right(high.at[e], low.at[e], tables, e)
+            stacked_halves(high, low, product, False)
+            for e in range(2):
+                far[m, e] = by_left(high.at[e], low.at[e], tables, 2 + e)
         for e in range(2):
-            power = 0.0
-            for m in range(2):
-                z = far[m, e]
-                power = power + z[:HALF] * z[:HALF] + z[HALF:] * z[HALF:]
-            factor = 1.0 - sorted_amps[p, e * HALF : (e + 1) * HALF] * jnp.minimum(
-                lax.rsqrt(power), 1.0 / floor_level
-            )
-            factor = rows(factor, factor)
-            for m in range(2):
-                far[m, e] = far[m, e] * factor
+            for r in range(0, HALF, STEP):
+                real, imag = pl.ds(r, STEP), pl.ds(HALF + r, STEP)
+                zs = [(far[m, e, real], far[m, e, imag]) for m in range(2)]
+                power = 0.0
+                for zr, zi in zs:
+                    power = power + (zr * zr + zi * zi)
+                amp = sorted_amps[p, e * HALF + r : e * HALF + r + STEP]
+                factor = 1.0 - amp * jnp.minimum(lax.rsqrt(power), 1.0 / floor_level)
+                for m, (zr, zi) in enumerate(zs):
+                    put(highs.at[m, e], lows.at[m, e], r, zr * factor)
+                    put(highs.at[m, e], lows.at[m, e], HALF + r, zi * factor)
         for m in range(2):
-            u = by_left(far[m, 0], tables, 4)
-            v = by_left(far[m, 1], tables, 5)
-            s, d = u + v, u - v
-            ie, io = halves(rows(s[:HALF], d[:HALF]), rows(s[HALF:], d[HALF:]))
-            u = by_right(ie, tables, 6)
-            v = by_right(io, tables, 7)
-            s, d = u + v, u - v
-            cr = lanes(s[:, :HALF], d[:, :HALF])
-            ci = lanes(s[:, HALF:], d[:, HALF:])
-            sr, si = patch[0], patch[1]
-            wr, wi = waves[p, 0, m].astype(f32), waves[p, 1, m].astype(f32)
-            gr, gi = wr * cr + wi * ci, wr * ci - wi * cr
-            if m == 0:
-                upd[p, 0], upd[p, 1] = gr, gi
-            else:
-                upd[p, 0], upd[p, 1] = upd[p, 0] + gr, upd[p, 1] + gi
-            back[p, m, 0] = sr * cr + si * ci
-            back[p, m, 1] = sr * ci - si * cr
+            high, low, product = highs.at[m], lows.at[m], products.at[m]
+            for e in range(2):
+                product[e] = by_left(high.at[e], low.at[e], tables, 4 + e)
+            for r in range(0, HALF, STEP):
+                real, imag = pl.ds(r, STEP), pl.ds(HALF + r, STEP)
+                ur, ui, vr, vi = product[0, real], product[0, imag], product[1, real], product[1, imag]
+                for at, re, im in ((r, ur + vr, ui + vi), (HALF + r, ur - vr, ui - vi)):
+                    even, odd = halves(re, im)
+                    put(high.at[0], low.at[0], at, even)
+                    put(high.at[1], low.at[1], at, odd)
+            for e in range(2):
+                product[e] = by_right(high.at[e], low.at[e], tables, 6 + e)
+            for r in range(0, PX, STEP):
+                part = pl.ds(r, STEP)
+                u, v = product[0, part], product[1, part]
+                s, d = u + v, u - v
+                cr = lanes(s[:, :HALF], d[:, :HALF])
+                ci = lanes(s[:, HALF:], d[:, HALF:])
+                sr, si = patch[0, part], patch[1, part]
+                wr, wi = waves[p, 0, m, part].astype(f32), waves[p, 1, m, part].astype(f32)
+                gr, gi = wr * cr + wi * ci, wr * ci - wi * cr
+                if m == 0:
+                    upd[p, 0, part], upd[p, 1, part] = gr, gi
+                else:
+                    upd[p, 0, part], upd[p, 1, part] = upd[p, 0, part] + gr, upd[p, 1, part] + gi
+                p0, p1 = halves(sr * cr + si * ci, sr * ci - si * cr)
+                put(back_high.at[p, m, 0], back_low.at[p, m, 0], r, p0 + p1)
+                put(back_high.at[p, m, 1], back_low.at[p, m, 1], r, p0 - p1)
         add_patch(p, 2, upd.at[p])
 
         @pl.when(p == 1)
@@ -402,65 +426,63 @@
     halo_one.wait()
     widen(0)
 
-    def phase_two(p, m):
-        if m == 0:
-            take_patch(p, upd.at[p])
-        p0, p1 = halves(back[p, m, 0], back[p, m, 1])
-        u = by_right(p0 + p1, tables, 8)
-        v = by_right(p0 - p1, tables, 9)
-        s, d = u + v, u - v
-        re = lanes(s[:, :HALF], d[:, :HALF])
-        im = lanes(s[:, HALF:], d[:, HALF:])
-        u = by_left(rows(re[:HALF] + re[HALF:], im[:HALF] + im[HALF:]), tables, 10)
-        v = by_left(rows(re[:HALF] - re[HALF:], im[:HALF] - im[HALF:]), tables, 11)
-        s, d = u + v, u - v
-        br = rows(s[:HALF], d[:HALF])
-        bi = rows(s[HALF:], d[HALF:])
-        pr, pi = probe[0, m], probe[1, m]
-        ar, ai = upd[p, 0], upd[p, 1]
-        gr, gi = pr * br + pi * bi, pr * bi - pi * br
-        for part, value in enumerate((ar * br + ai * bi, ar * bi - ai * br)):
-            for h in range(2):
-                half = value[:, h * HALF : (h + 1) * HALF].reshape(16, 2, 8, HALF)
-                gp[m, h, part] = gp[m, h, part] + half
-        if m == 0:
-            back[p, 0, 0], back[p, 0, 1] = gr, gi
-        else:
-            patch[0], patch[1] = back[p, 0, 0] + gr, back[p, 0, 1] + gi
-            add_patch(p, 0, patch)
-
-    def first_mode(p, carry):
-        phase_two(p, 0)
+    def phase_two(p, carry):
+        take_patch(p, patch)
+        for m in range(2):
+            high, low, product = highs.at[m], lows.at[m], products.at[m]
+            for e in range(2):
+                product[e] = by_right(back_high.at[p, m, e], back_low.at[p, m, e], tables, 8 + e)
+            stacked_halves(high, low, product, True)
+            for e in range(2):
+                far[m, e] = by_left(high.at[e], low.at[e], tables, 10 + e)
+        for r in range(0, HALF, STEP):
+            real, imag = pl.ds(r, STEP), pl.ds(HALF + r, STEP)
+            for bottom in range(2):
+                part = pl.ds(bottom * HALF + r, STEP)
+                ar, ai = patch[0, part], patch[1, part]
+                sum_r, sum_i = 0.0, 0.0
+                for m in range(2):
+                    ur, ui, vr, vi = far[m, 0, real], far[m, 0, imag], far[m, 1, real], far[m, 1, imag]
+                    br, bi = (ur - vr, ui - vi) if bottom else (ur + vr, ui + vi)
+                    pr, pi = probe[0, m, part], probe[1, m, part]
+                    sum_r = sum_r + (pr * br + pi * bi)
+                    sum_i = sum_i + (pr * bi - pi * br)
+                    tile_at = (bottom * HALF + r) // 16
+                    for c, value in enumerate((ar * br + ai * bi, ar * bi - ai * br)):
+                        for h in range(2):
+                            half = value[:, h * HALF : (h + 1) * HALF].reshape(STEP // 16, 2, 8, HALF)
+                            for l in range(2):
+                                to = c * 2 + m, l * 2 + h, pl.ds(tile_at, STEP // 16)
+                                gp[to] = gp[to] + half[:, l]
+                upd[p, 0, part], upd[p, 1, part] = sum_r, sum_i
         return carry
 
-    def second_mode(p, carry):
-        phase_two(p, 1)
+    def scatter_one(p, carry):
+        add_patch(p, 0, upd.at[p])
         return carry
-
-    def stage_one(m):
-        return [send(gp.at[m, 1 - core], r1.at[m], pair_sems.at[0, m], other_core)]
-
-    def stage_two(m):
-        for l in range(2):
-            s1[m, l] = gp[m, core, :, :, l] + r1[m, :, :, l]
-        return [send(s1.at[m, 1 - layer], r2.at[m], pair_sems.at[1, m], other_layer)]
 
     def finish(copies):
         for copy in copies:
             copy.wait()
 
-    lax.fori_loop(0, POSITIONS, first_mode, 0)
-    one_a = stage_one(0)
+    def code_piece(q, carry):
+        values = gp[q // 4, q % 4].reshape(HALF, HALF)
+        largest = jnp.maximum(jnp.max(jnp.abs(values), axis=0, keepdims=True), 1e-30)
+        power = jnp.ceil(jnp.log2(largest))
+        scaled = values * (LEVELS_TWO * jnp.exp2(-power))
+        probe_codes[q, :HALF] = jnp.round(scaled).astype(jnp.int32).astype(jnp.int16)
+        probe_codes[q, HALF:] = jnp.broadcast_to(power, (16, HALF)).astype(jnp.int32).astype(jnp.int16)
+        return carry
+
+    lax.fori_loop(0, 1, phase_two, 0)
     rim_two.forward()
-    lax.fori_loop(0, 1, second_mode, 0)
-    finish(one_a)
-    two_a = stage_two(0)
-    lax.fori_loop(1, POSITIONS, second_mode, 0)
-    one_b = stage_one(1)
+    lax.fori_loop(1, POSITIONS, phase_two, 0)
+    lax.fori_loop(0, 16, code_piece, 0)
+    one = [
+        send(probe_codes.at[(spot + j) % 16], r1.at[j - 1], sems3.at[j - 1], along_spot(j)) for j in range(1, 16)
+    ]
+    lax.fori_loop(0, POSITIONS, scatter_one, 0)
     scale_one = send_rims(rim_one)
-    finish(two_a)
-    finish(one_b)
-    two_b = stage_two(1)
     rim_two.wait()
     finish(scale_two)
     rim_one.forward()
@@ -478,15 +500,13 @@
 
     for c in (2, 3):
         acc = total_of(c, acc)
-    finish(two_b)
-    for m in range(2):
-        for part in range(2):
-            s2[part * 2 + m] = s1[m, layer, part] + r2[m, part]
-    copies = []
-    for j in range(1, 4):
-        copies.append(send(s2.at[(x + j) % 4], r3.at[j - 1], sems3.at[j - 1], along_x(j)))
-    finish(copies)
-    s3[...] = s2[x] + r3[0] + r3[1] + r3[2]
+    finish(one)
+    mine = gp[x, g]
+    for j in range(15):
+        power = r1[j, HALF:].astype(jnp.int32).astype(f32)[:1]
+        codes = r1[j, :HALF].astype(jnp.int32).astype(f32)
+        mine = mine + (codes * (jnp.exp2(power) * (1.0 / LEVELS_TWO))).reshape(16, 8, HALF)
+    s3[...] = mine
     four = [send(s3.at[(zy + j) % 16], r4.at[j - 1], sems4.at[j - 1], along_zy(j)) for j in range(1, 16)]
     rim_one.wait()
     finish(scale_one)
@@ -553,29 +573,30 @@
             pltpu.VMEM((2, ROWS + PX, 3 * HALF), f32),
             pltpu.VMEM((2, *whole), f32),
             pltpu.VMEM((2, 2, *whole), f32),
-            pltpu.VMEM((3, 2, 2, *whole), f32),
+            pltpu.VMEM((3, 2, 2, *whole), bf16),
+            pltpu.VMEM((3, 2, 2, *whole), bf16),
+            pltpu.VMEM((2, 2, *whole), bf16),
+            pltpu.VMEM((2, 2, *whole), bf16),
+            pltpu.VMEM((2, 2, *whole), f32),
             pltpu.VMEM((3, 2, *whole), f32),
             pltpu.VMEM((3, *whole), f32),
-            pltpu.VMEM((2, 2, 2, 16, 2, *tile), f32),
+            pltpu.VMEM((4, 4, 16, *tile), f32),
             pltpu.VMEM((2, 4, ROWS, HALF), jnp.int16),
             pltpu.VMEM((2, 4, *tile), f32),
             pltpu.VMEM((2, 4, ROWS, HALF), jnp.int16),
             pltpu.VMEM((2, 4, *tile), f32),
             pltpu.VMEM((2, 2, ROWS, HALF), bf16),
             pltpu.VMEM((2, 2, ROWS, HALF), jnp.int16),
-            pltpu.VMEM((2, 2, 16, 2, *tile), f32),
-            pltpu.VMEM((2, 2, 2, 16, *tile), f32),
-            pltpu.VMEM((2, 2, 16, *tile), f32),
-            pltpu.VMEM((4, 16, *tile), f32),
-            pltpu.VMEM((3, 16, *tile), f32),
+            pltpu.VMEM((16, HALF + 16, HALF), jnp.int16),
+            pltpu.VMEM((15, HALF + 16, HALF), jnp.int16),
             pltpu.VMEM((16, *tile), f32),
             pltpu.VMEM((15, *tile), f32),
             pltpu.VMEM((4, *tile), f32),
             pltpu.VMEM((16, *tile), f32),
             pltpu.VMEM((16, *tile), f32),
             sem((4,)), sem((4, 2, 2)), sem((4, 2, PIECES, 2)), sem((4, 2, PIECES, 2)), sem((4, 2, PIECES)),
-            sem((2, 2, 2)), sem((2, 2, 2)),
-            sem((3, 2)), sem((15, 2)), sem((3, 2)), sem((15, 2)), sem((15, 2)),
+            sem((2, 2, 2)),
+            sem((15, 2)), sem((15, 2)), sem((3, 2)), sem((15, 2)), sem((15, 2)),
         ],
         compiler_params=pltpu.CompilerParams(
             collective_id=0, has_side_effects=True, vmem_limit_bytes=56 * 1024 * 1024

time: 88.3 us -> 85.1 us (0.964)
  Pallas kernels: 84.8 us -> 81.5 us
    pallas_call x1, Pallas kernels: 83.6 us -> 80.4 us  [shards(): pl.pallas_call(kernel, out_shape=[strip, jax.ShapeDtypeStruct(tile, f32),...]
where the time goes in v4:
time: 85.1 us; the launch traced here: 84.8 us
  Pallas kernels  81.5 us (96%)
  local copies, waits for them, and re-layouts  2.62 us (3%)
    pallas_call x1, Pallas kernels, shards(): pl.pallas_call(kernel, out_shape=[strip, jax.ShapeDtypeStruct(tile, f32),...  80.4 us
    unnamed x10, local copies, waits for them, and re-layouts  2.62 us

profile of v4, /device:TPU:1, one launch (start us, length us, event | category | flops | bytes accessed | tf_op | source)
XLA Modules:
  0.0 84.8 jit_solution(13150134290195947336)
XLA Ops:
  0.6 0.0 copy-start
  0.6 0.0 copy-start.1
  0.7 80.4 %update.1 = (f32[4,512,128]{2,1,0:T(8,128)}, f32[8,128]{1,0:T(8,128)}, f32[16,256]{1,0:T(8,128)}) custom-call(s32[3]{0:T(128)} %bitcast.8, s32[3]{0:T(128)} %bitcast.9, bf16[4,512,128]{2,1,0:T(8,128)(2,1)} %own_obj.3, f32[2,2,256,256]{3,2,1,0:T(8,128)} %bitcast.5, bf16[3,2,2,256,256]{4,3,2,1,0:T(8,128)(2,1)} %bitcast.6, bf16[3,256,256]{2,1,0:T(8,128)(2,1)} %bitcast.7, ...), custom_call_target="tpu_custom_call" | custom-call | tf_op jit(solution)/shard_map/update/pallas_call | solution.py:560
  81.0 0.0 copy-done
  81.0 0.0 copy-done.1
  81.1 0.0 copy-start.2
  81.1 1.2 %copy-done.2 = f32[4,512,128]{2,1,0:T(8,128)S(1)} copy-done((f32[4,512,128]{2,1,0:T(8,128)S(1)}, f32[4,512,128]{2,1,0:T(8,128)}, u32[]{:S(2)}) %copy-start.2) | copy-done | bytes 1048600
  82.3 0.0 copy-start.3
  82.3 0.7 copy-done.3
  83.0 0.0 copy-start.4
  83.0 0.7 copy-done.4
  83.7 1.2 %final.1 = (f32[4,512,128]{2,1,0:T(8,128)}, f32[16,256]{1,0:T(8,128)}) custom-call(bf16[4,512,128]{2,1,0:T(8,128)(2,1)S(1)} %copy-done.1, f32[4,512,128]{2,1,0:T(8,128)S(1)} %copy-done.2, f32[8,128]{1,0:T(8,128)S(1)} %copy-done.4, f32[16,256]{1,0:T(8,128)S(1)} %copy-done.3, f32[1024,256]{1,0:T(8,128)S(1)} %copy-done), custom_call_target="tpu_custom_call" | custom-call | tf_op jit(solution)/shard_map/final/pallas_call | solution.py:609
Async XLA Ops:
  0.6 80.4 %copy-start = (f32[1024,256]{1,0:T(8,128)S(1)}, f32[1024,256]{1,0:T(8,128)}, u32[]{:S(2)}) copy-start(f32[1024,256]{1,0:T(8,128)} %old_probe.1) | copy-start | bytes 3145732
  0.6 80.4 %copy-start.1 = (bf16[4,512,128]{2,1,0:T(8,128)(2,1)S(1)}, bf16[4,512,128]{2,1,0:T(8,128)(2,1)}, u32[]{:S(2)}) copy-start(bf16[4,512,128]{2,1,0:T(8,128)(2,1)} %own_obj.3) | copy-start | bytes 1572868
  81.1 1.2 %copy-start.2 = (f32[4,512,128]{2,1,0:T(8,128)S(1)}, f32[4,512,128]{2,1,0:T(8,128)}, u32[]{:S(2)}) copy-start(f32[4,512,128]{2,1,0:T(8,128)} %get-tuple-element.5.total) | copy-start | bytes 3145732
  82.3 0.7 copy-start.3
  83.0 0.7 copy-start.4

commit v5 on v4

--- a/solution.py
+++ b/solution.py
@@ -20,7 +20,7 @@
 ROWS = 512
 POSITIONS = 3
 CHUNKS = 8
-PIECES = 4
+PIECES = 2
 STEP = 32
 CHUNK_ROWS = ROWS // PIECES
 LEVELS = 32767.0
@@ -483,9 +483,9 @@
     ]
     lax.fori_loop(0, POSITIONS, scatter_one, 0)
     scale_one = send_rims(rim_one)
+    rim_one.forward()
     rim_two.wait()
     finish(scale_two)
-    rim_one.forward()
     acc = jnp.zeros((8, HALF), f32)
 
     def total_of(c, acc):
@@ -537,14 +537,26 @@
         shard_out[s // 2 * 8 : s // 2 * 8 + 8, s % 2 * HALF : s % 2 * HALF + HALF] = fin[(g + 4 - s) % 4]
 
 
-def final_kernel(own_obj, total, squares, shard, old_probe, object_new, probe_new):
+def final_kernel(own_hbm, total_hbm, squares_hbm, shard_hbm, probe_hbm, object_new, probe_new,
+                 own_obj, total, squares, shard, old_probe, sems):
+    at = pl.multiple_of(lax.axis_index("tile") * 16, 16)
+    loads = [
+        pltpu.make_async_copy(src, dst, sems.at[i])
+        for i, (src, dst) in enumerate([
+            (squares_hbm, squares), (total_hbm, total), (own_hbm, own_obj), (shard_hbm, shard),
+            (probe_hbm.at[pl.ds(at, 16)], old_probe),
+        ])
+    ]
+    for load in loads:
+        load.start()
+    for load in loads:
+        load.wait()
     sums = jnp.sum(squares[...], axis=1, keepdims=True)
     object_step_size = object_step * lax.rsqrt(sums[0:1] * (1.0 / OBJECT_COUNT) + epsilon)
     probe_step_size = probe_step * lax.rsqrt(sums[4:5] * (1.0 / PROBE_COUNT) + epsilon)
     for c in range(4):
         object_new[c] = own_obj[c].astype(f32) - total[c] * object_step_size
-    at = pl.multiple_of(lax.axis_index("tile") * 16, 16)
-    probe_new[...] = old_probe[pl.ds(at, 16), :] - shard[...] * probe_step_size
+    probe_new[...] = old_probe[...] - shard[...] * probe_step_size
 
 
 def shards(object_slices, probe, mid_waves, amplitudes, row_offsets, col_offsets):
@@ -609,8 +621,12 @@
     return pl.pallas_call(
         final_kernel,
         out_shape=[strip, shard],
-        in_specs=[vmem] * 5,
+        in_specs=[anywhere] * 5,
         out_specs=[vmem] * 2,
+        scratch_shapes=[
+            pltpu.VMEM(object_slices.shape, bf16), pltpu.VMEM(object_slices.shape, f32), pltpu.VMEM(tile, f32),
+            pltpu.VMEM((16, PX), f32), pltpu.VMEM((16, PX), f32), sem((5,)),
+        ],
         compiler_params=pltpu.CompilerParams(vmem_limit_bytes=16 * 1024 * 1024),
         name="final",
     )(object_slices, total, squares, shard_sum, probe)

time: 85.1 us -> 84.8 us (level)
  no operation moved by 1% of the time
where the time goes in v5:
time: 84.8 us; the launch traced here: 84.5 us
  Pallas kernels  81.2 us (96%)
  local copies, waits for them, and re-layouts  2.62 us (3%)
    pallas_call x1, Pallas kernels, shards(): pl.pallas_call(kernel, out_shape=[strip, jax.ShapeDtypeStruct(tile, f32),...  79.8 us
    unnamed x10, local copies, waits for them, and re-layouts  2.62 us

profile of v5, /device:TPU:1, one launch (start us, length us, event | category | flops | bytes accessed | tf_op | source)
XLA Modules:
  0.0 84.5 jit_solution(5802954468064870761)
XLA Ops:
  0.6 0.0 copy-start
  0.6 0.0 copy-start.1
  0.7 79.8 %update.1 = (f32[4,512,128]{2,1,0:T(8,128)}, f32[8,128]{1,0:T(8,128)}, f32[16,256]{1,0:T(8,128)}) custom-call(s32[3]{0:T(128)} %bitcast.8, s32[3]{0:T(128)} %bitcast.9, bf16[4,512,128]{2,1,0:T(8,128)(2,1)} %own_hbm.1, f32[2,2,256,256]{3,2,1,0:T(8,128)} %bitcast.5, bf16[3,2,2,256,256]{4,3,2,1,0:T(8,128)(2,1)} %bitcast.6, bf16[3,256,256]{2,1,0:T(8,128)(2,1)} %bitcast.7, ...), custom_call_target="tpu_custom_call" | custom-call | tf_op jit(solution)/shard_map/update/pallas_call | solution.py:572
  80.5 0.0 copy-done
  80.5 0.0 copy-done.1
  80.5 0.0 copy-start.2
  80.5 1.2 %copy-done.2 = f32[4,512,128]{2,1,0:T(8,128)S(1)} copy-done((f32[4,512,128]{2,1,0:T(8,128)S(1)}, f32[4,512,128]{2,1,0:T(8,128)}, u32[]{:S(2)}) %copy-start.2) | copy-done | bytes 1048600
  81.7 0.0 copy-start.3
  81.7 0.7 copy-done.3
  82.5 0.0 copy-start.4
  82.5 0.7 copy-done.4
  83.1 1.4 %final.1 = (f32[4,512,128]{2,1,0:T(8,128)}, f32[16,256]{1,0:T(8,128)}) custom-call(bf16[4,512,128]{2,1,0:T(8,128)(2,1)S(1)} %copy-done.1, f32[4,512,128]{2,1,0:T(8,128)S(1)} %copy-done.2, f32[8,128]{1,0:T(8,128)S(1)} %copy-done.4, f32[16,256]{1,0:T(8,128)S(1)} %copy-done.3, f32[1024,256]{1,0:T(8,128)S(1)} %copy-done), custom_call_target="tpu_custom_call" | custom-call | tf_op jit(solution)/shard_map/final/pallas_call | solution.py:621
Async XLA Ops:
  0.6 79.9 %copy-start = (f32[1024,256]{1,0:T(8,128)S(1)}, f32[1024,256]{1,0:T(8,128)}, u32[]{:S(2)}) copy-start(f32[1024,256]{1,0:T(8,128)} %probe_hbm.1) | copy-start | bytes 3145732
  0.6 79.9 %copy-start.1 = (bf16[4,512,128]{2,1,0:T(8,128)(2,1)S(1)}, bf16[4,512,128]{2,1,0:T(8,128)(2,1)}, u32[]{:S(2)}) copy-start(bf16[4,512,128]{2,1,0:T(8,128)(2,1)} %own_hbm.1) | copy-start | bytes 1572868
  80.5 1.2 %copy-start.2 = (f32[4,512,128]{2,1,0:T(8,128)S(1)}, f32[4,512,128]{2,1,0:T(8,128)}, u32[]{:S(2)}) copy-start(f32[4,512,128]{2,1,0:T(8,128)} %get-tuple-element.5.total_hbm) | copy-start | bytes 3145732
  81.7 0.7 copy-start.3
  82.5 0.7 copy-start.4
